TPU v7x, 32 devices: a whole 2x2x4 slice. The times are simulated.
32 devices in a mesh: dp: 8 (over z, y), tensor: 4 (over x, core).
Axes of the slice: x: 2, y: 2, z: 4, core: 2. Of those that a mesh axis runs over, the one named last changes fastest.
Arguments:
- tokens: bfloat16 [8192, 768], P(('dp', 'tensor')), may hold values from -6 to 6
- cotangent: bfloat16 [8192, 768], P(('dp', 'tensor')), may hold values from -6 to 6
- lengths: int32 [8], P('dp'), may hold values from 128 to 1024, as said below
- attn_w: float32 [4, 768, 768], P('tensor', 'dp')
- up_w: float32 [768, 3072], P('dp', 'tensor'), may hold values from -0.21875 to 0.21875
- down_w: float32 [3072, 768], P('tensor', 'dp'), may hold values from -0.109375 to 0.109375
- norm_params: float32 [4, 768], replicated, may hold values from -2 to 2
- attn_mom: float32 [4, 768, 768], P('tensor', 'dp')
- up_mom: float32 [768, 3072], P('dp', 'tensor')
- down_mom: float32 [3072, 768], P('tensor', 'dp')
- norm_m1: float32 [4, 768], replicated
- norm_m2: float32 [4, 768], replicated, may hold values from 204 to 910
Outputs:
- mixed: bfloat16 [8192, 768], P(('dp', 'tensor'))
- input_grad: float32 [8192, 768], P(('dp', 'tensor'))
- attn_new: float32 [4, 768, 768], P('tensor', 'dp')
- attn_moment: float32 [4, 768, 768], P('tensor', 'dp')
- up_new: float32 [768, 3072], P('dp', 'tensor')
- up_moment: float32 [768, 3072], P('dp', 'tensor')
- down_new: float32 [3072, 768], P('tensor', 'dp')
- down_moment: float32 [3072, 768], P('tensor', 'dp')
- norm_moment1: float32 [4, 768], replicated
- norm_moment2: float32 [4, 768], replicated
- norm_new: float32 [4, 768], replicated
Inputs may be any that keep to these rules, and one draw needn't show every extreme that they name: `lengths`: some sequence has exactly 1024 true positions.
All inputs are finite; a program needn't handle non-finite values.
Results may differ from a plain program's by a relative error of at most 0.017.
Values may be sent and summed in bfloat16 or wider, within the bound.
A program may use at most 192 MiB of HBM per device.

v0:
```python
import math

import jax
import jax.numpy as jnp
from jax import lax
from jax.sharding import PartitionSpec as P

HEADS = 12
HDIM = 64
BLOCK = 64
NS_STEPS = 5
STEP = 10


NORM_EPS = 1e-05
NS_EPS = 1e-07
COEF_A = 3.4445
COEF_B = -4.775
COEF_C = 2.0315
MUON_RATE = 0.15
MUON_DECAY = 0.1
ADAM_RATE = 0.2


def cut_along(array, dim, size):
    lengths = array.shape
    pieces = array.reshape(*lengths[:dim], size, lengths[dim] // size, *lengths[dim + 1 :])
    return jnp.moveaxis(pieces, dim, 0)


def sum_at_owner(array, axis, dim):
    size = lax.axis_size(axis)
    pieces = lax.all_to_all(cut_along(array, dim, size), axis, 0, 0, tiled=True)
    return jnp.sum(pieces.astype(jnp.float32), axis=0)


def sent_together(arrays, axis, dim, along):
    widths = [a.shape[along] for a in arrays]
    both = jnp.concatenate(arrays, axis=along)
    whole = sum_at_owner(both, axis, dim)
    return tuple(jnp.split(whole, [sum(widths[:k]) for k in range(1, len(widths))], axis=along))


def partner(array, axis, bit):
    return lax.ppermute(array, axis, [(i, i ^ 1 << bit) for i in range(lax.axis_size(axis))])


def contract_rows(left, right):
    return lax.dot_general(
        left, right, (((0,), (0,)), ((), ())), preferred_element_type=jnp.float32
    )


def contract_cols(left, right):
    return lax.dot_general(
        left, right, (((1,), (1,)), ((), ())), preferred_element_type=jnp.float32
    )


def norm_forward(resid, gain, bias):
    center = resid - jnp.mean(resid, -1, keepdims=True)
    spread = jnp.mean(center * center, -1, keepdims=True)
    scale_inv = lax.rsqrt(spread + NORM_EPS)
    normal_rows = center * scale_inv
    return (normal_rows, scale_inv, normal_rows * gain + bias)


def norm_back(normal_rows, scale_inv, grad_normed):
    return scale_inv * (
        grad_normed
        - jnp.mean(grad_normed, -1, keepdims=True)
        - normal_rows * jnp.mean(grad_normed * normal_rows, -1, keepdims=True)
    )


def smooth_gate(values):
    return jax.nn.gelu(values, approximate=True)


def features(proj, cosine, sine, weight_rows):
    count = proj.shape[0]
    soft = jax.nn.softplus(proj).reshape(count, HEADS, HDIM)
    both = jnp.concatenate([soft * cosine[:, None, None], soft * sine[:, None, None]], -1)
    return both * weight_rows[:, None, None]


def features_back(grad_feat, proj, cosine, sine, weight_rows):
    count = proj.shape[0]
    grad_soft = (
        grad_feat[..., :HDIM] * cosine[:, None, None] + grad_feat[..., HDIM:] * sine[:, None, None]
    )
    grad_soft = grad_soft * weight_rows[:, None, None]
    slope = jax.nn.sigmoid(proj).reshape(count, HEADS, HDIM)
    return (grad_soft * slope).reshape(count, HEADS * HDIM).astype(jnp.bfloat16)


def blocked(array):
    return array.reshape(array.shape[0] // BLOCK, BLOCK, array.shape[1], array.shape[2])


def attend_forward(qblock, kblock, vblock, lower):
    scores = (
        jnp.einsum("nihf,njhf->nhij", qblock, kblock, preferred_element_type=jnp.float32) * lower
    )
    scores_low = scores.astype(jnp.bfloat16)
    pairs = jnp.einsum("njhf,njhd->nhfd", kblock, vblock, preferred_element_type=jnp.float32)
    state = jnp.cumsum(pairs, 0) - pairs
    state_low = state.astype(jnp.bfloat16)
    key_sum = jnp.sum(kblock.astype(jnp.float32), 1)
    zsum = jnp.cumsum(key_sum, 0) - key_sum
    numer = jnp.einsum("nhij,njhd->nihd", scores_low, vblock, preferred_element_type=jnp.float32)
    numer = numer + jnp.einsum(
        "nihf,nhfd->nihd", qblock, state_low, preferred_element_type=jnp.float32
    )
    denom = jnp.transpose(jnp.sum(scores, -1), (0, 2, 1))
    denom = denom + jnp.einsum(
        "nihf,nhf->nih", qblock.astype(jnp.float32), zsum, precision=lax.Precision.HIGHEST
    )
    return (scores_low, state_low, zsum, denom, numer / denom[..., None])


def attend_backward(
    qblock, kblock, vblock, lower, scores_low, state_low, zsum, denom, result, grad_out
):
    grad_numer = (grad_out / denom[..., None]).astype(jnp.bfloat16)
    grad_denom = -jnp.sum(grad_out * result, -1) / denom
    grad_scores = jnp.einsum(
        "nihd,njhd->nhij", grad_numer, vblock, preferred_element_type=jnp.float32
    )
    grad_scores = ((grad_scores + jnp.transpose(grad_denom, (0, 2, 1))[..., None]) * lower).astype(
        jnp.bfloat16
    )
    grad_state = jnp.einsum(
        "nihf,nihd->nhfd", qblock, grad_numer, preferred_element_type=jnp.float32
    )
    grad_pairs = (jnp.cumsum(grad_state[::-1], 0)[::-1] - grad_state).astype(jnp.bfloat16)
    grad_z = jnp.einsum(
        "nih,nihf->nhf", grad_denom, qblock.astype(jnp.float32), precision=lax.Precision.HIGHEST
    )
    grad_ksum = jnp.cumsum(grad_z[::-1], 0)[::-1] - grad_z
    grad_qf = jnp.einsum("nhij,njhf->nihf", grad_scores, kblock, preferred_element_type=jnp.float32)
    grad_qf = grad_qf + jnp.einsum(
        "nihd,nhfd->nihf", grad_numer, state_low, preferred_element_type=jnp.float32
    )
    grad_qf = grad_qf + grad_denom[..., None] * zsum[:, None]
    grad_kf = jnp.einsum("nhij,nihf->njhf", grad_scores, qblock, preferred_element_type=jnp.float32)
    grad_kf = grad_kf + jnp.einsum(
        "njhd,nhfd->njhf", vblock, grad_pairs, preferred_element_type=jnp.float32
    )
    grad_kf = grad_kf + grad_ksum[:, None]
    grad_val = jnp.einsum(
        "nhij,nihd->njhd", scores_low, grad_numer, preferred_element_type=jnp.float32
    )
    grad_val = grad_val + jnp.einsum(
        "njhf,nhfd->njhd", kblock, grad_pairs, preferred_element_type=jnp.float32
    )
    return (grad_qf, grad_kf, grad_val.astype(jnp.bfloat16))


def newton_update(iterate, gram):
    poly = (
        COEF_B * gram.astype(jnp.float32)
        + COEF_C * jnp.dot(gram, gram, preferred_element_type=jnp.float32)
    ).astype(jnp.bfloat16)
    return (
        COEF_A * iterate.astype(jnp.float32)
        + jnp.dot(poly, iterate, preferred_element_type=jnp.float32)
    ).astype(jnp.bfloat16)


def orthogonalize(iterate):
    for step in range(NS_STEPS):
        gram = jnp.dot(iterate, iterate.T, preferred_element_type=jnp.float32).astype(jnp.bfloat16)
        iterate = newton_update(iterate, gram)
    return iterate


def on_device(
    tokens,
    cotangent,
    lengths,
    attn_w,
    up_w,
    down_w,
    norm_params,
    attn_mom,
    up_mom,
    down_mom,
    norm_m1,
    norm_m2,
):
    tensor_index = lax.axis_index("tensor")
    data_index = lax.axis_index("dp")
    tensor_count = lax.axis_size("tensor")
    length = lengths[0]
    rows_here = tokens.shape[0]
    wa_rows, up_block, down_block = (
        lax.all_gather(attn_w.astype(jnp.bfloat16), "dp", axis=1, tiled=True),
        lax.all_gather(up_w.astype(jnp.bfloat16), "dp", axis=0, tiled=True),
        lax.all_gather(down_w.astype(jnp.bfloat16), "dp", axis=1, tiled=True),
    )
    w_all = lax.all_gather(wa_rows, "tensor", axis=0, tiled=True)
    w_query = w_all[0]
    w_key = w_all[1]
    w_value = w_all[2]
    w_out = w_all[3]
    sequence = lax.all_gather(tokens, "tensor", axis=0, tiled=True)
    count = sequence.shape[0]
    width = sequence.shape[1]
    blocks = count // BLOCK
    start_row = tensor_index * rows_here

    def mine(array):
        return lax.dynamic_slice_in_dim(array, start_row, rows_here, 0)

    where = jnp.arange(count)
    live = (where < length).astype(jnp.float32)
    place = jnp.minimum(where, length - 1).astype(jnp.float32)
    theta = 0.5 * math.pi * place / length.astype(jnp.float32)
    cosine = jnp.cos(theta)
    sine = jnp.sin(theta)
    every_row = jnp.ones((count,), jnp.float32)
    query = jnp.dot(sequence, w_query, preferred_element_type=jnp.float32)
    key_proj = jnp.dot(sequence, w_key, preferred_element_type=jnp.float32)
    value = jnp.dot(sequence, w_value, preferred_element_type=jnp.float32)
    qblock = blocked(features(query, cosine, sine, every_row).astype(jnp.bfloat16))
    kblock = blocked(features(key_proj, cosine, sine, live).astype(jnp.bfloat16))
    vblock = value.astype(jnp.bfloat16).reshape(blocks, BLOCK, HEADS, HDIM)
    lower = jnp.tril(jnp.ones((BLOCK, BLOCK), jnp.float32))
    scores_low, state_low, zsum, denom, result = attend_forward(qblock, kblock, vblock, lower)
    attn_low = result.reshape(count, width).astype(jnp.bfloat16)
    branch = jnp.dot(attn_low, w_out, preferred_element_type=jnp.float32)
    normal_one, scale_one, hidden_in = norm_forward(
        sequence.astype(jnp.float32) + branch, norm_params[0], norm_params[1]
    )
    hidden_low = hidden_in.astype(jnp.bfloat16)
    pre = jnp.dot(hidden_low, up_block, preferred_element_type=jnp.float32)
    act_low = smooth_gate(pre).astype(jnp.bfloat16)
    ffn_rows = lax.psum_scatter(
        jnp.dot(act_low, down_block, preferred_element_type=jnp.float32).astype(jnp.bfloat16),
        "tensor",
        scatter_dimension=0,
        tiled=True,
    ).astype(jnp.float32)
    live_rows = mine(live)
    normal_two, scale_two, normed = norm_forward(
        mine(hidden_in) + ffn_rows, norm_params[2], norm_params[3]
    )
    mixed = (live_rows[:, None] * normed).astype(jnp.bfloat16)
    grad_y = cotangent.astype(jnp.float32) * live_rows[:, None]
    grad_g2 = jnp.sum(grad_y * normal_two, 0)
    grad_b2 = jnp.sum(grad_y, 0)
    grad_r2 = norm_back(normal_two, scale_two, grad_y * norm_params[2])
    grad_r2_all = lax.all_gather(grad_r2.astype(jnp.bfloat16), "tensor", axis=0, tiled=True)
    grad_down = contract_rows(act_low, grad_r2_all)
    grad_act = contract_cols(grad_r2_all, down_block)
    gate_out, gate_pull = jax.vjp(smooth_gate, pre)
    grad_pre = gate_pull(grad_act)[0].astype(jnp.bfloat16)
    grad_up = contract_rows(hidden_low, grad_pre)
    grad_hidden = (
        lax.psum_scatter(
            contract_cols(grad_pre, up_block).astype(jnp.bfloat16),
            "tensor",
            scatter_dimension=0,
            tiled=True,
        ).astype(jnp.float32)
        + grad_r2
    )
    normal_one_rows = mine(normal_one)
    grad_g1 = jnp.sum(grad_hidden * normal_one_rows, 0)
    grad_b1 = jnp.sum(grad_hidden, 0)
    grad_r1 = norm_back(normal_one_rows, mine(scale_one), grad_hidden * norm_params[0])
    grad_branch = lax.all_gather(grad_r1.astype(jnp.bfloat16), "tensor", axis=0, tiled=True)
    grad_attn = contract_cols(grad_branch, w_out).reshape(blocks, BLOCK, HEADS, HDIM)
    grad_qf, grad_kf, grad_val = attend_backward(
        qblock, kblock, vblock, lower, scores_low, state_low, zsum, denom, result, grad_attn
    )
    grad_query = features_back(
        grad_qf.reshape(count, HEADS, 2 * HDIM), query, cosine, sine, every_row
    )
    grad_key = features_back(grad_kf.reshape(count, HEADS, 2 * HDIM), key_proj, cosine, sine, live)
    grad_value = grad_val.reshape(count, width)
    input_grad = (
        grad_r1
        + contract_cols(mine(grad_query), w_query)
        + contract_cols(mine(grad_key), w_key)
        + contract_cols(mine(grad_value), w_value)
    )
    left_rows = jnp.where(tensor_index == 3, attn_low, sequence)
    right_all = jnp.stack((grad_query, grad_key, grad_value, grad_branch))
    right_rows = lax.dynamic_index_in_dim(right_all, tensor_index, 0, keepdims=False)
    grad_owned = contract_rows(left_rows, right_rows)
    norm_partial = jnp.stack((grad_g1, grad_b1, grad_g2, grad_b2))
    grad_a, grad_u, grad_d = (
        *sent_together((grad_owned.astype(jnp.bfloat16), grad_up.astype(jnp.bfloat16)), "dp", 0, 1),
        sum_at_owner(grad_down.astype(jnp.bfloat16), "dp", 1),
    )
    moment_a = 0.5 * attn_mom[0] + grad_a
    moment_u = 0.5 * up_mom + grad_u
    moment_d = 0.5 * down_mom + grad_d
    owner_pick = jax.nn.one_hot(tensor_index, 4, dtype=jnp.float32)
    squares = jnp.concatenate(
        (
            owner_pick * jnp.sum(moment_a * moment_a),
            jnp.stack((jnp.sum(moment_u * moment_u), jnp.sum(moment_d * moment_d))),
        )
    )
    totals, norm_grad = lax.psum((squares, norm_partial), ("dp", "tensor"))
    size_a = jnp.sqrt(jnp.sum(totals[:4] * owner_pick))
    size_u = jnp.sqrt(totals[4])
    size_d = jnp.sqrt(totals[5])
    start_a = (moment_a / (size_a + NS_EPS)).astype(jnp.bfloat16)
    start_u = (moment_u / (size_u + NS_EPS)).astype(jnp.bfloat16)
    start_d = (moment_d.T / (size_d + NS_EPS)).astype(jnp.bfloat16)
    whole_a, cols_u, cols_d = (
        lax.all_gather(start_a, "dp", axis=0, tiled=True),
        lax.all_gather(start_u, "dp", axis=0, tiled=True),
        lax.all_gather(start_d, "dp", axis=0, tiled=True),
    )
    orth_a = orthogonalize(whole_a)
    is_even = tensor_index % 2 == 0
    whole_u, whole_d = (
        lax.all_gather(cols_u, "tensor", axis=1, tiled=True),
        lax.all_gather(cols_d, "tensor", axis=1, tiled=True),
    )
    orth_whole = orthogonalize(jnp.where(is_even, whole_u, whole_d))
    block_cols = cols_u.shape[1]
    own_block = lax.dynamic_slice_in_dim(orth_whole, tensor_index * block_cols, block_cols, 1)
    partner_block = lax.dynamic_slice_in_dim(
        orth_whole, jnp.bitwise_xor(tensor_index, 1) * block_cols, block_cols, 1
    )
    fetched = partner(partner_block, "tensor", 0)
    orth_u = jnp.where(is_even, own_block, fetched)
    orth_d = jnp.where(is_even, fetched, own_block)
    span = moment_a.shape[0]

    def take_rows(array):
        return lax.dynamic_slice_in_dim(array, data_index * span, span, 0).astype(jnp.float32)

    ff_whole = up_block.shape[1] * tensor_count
    keep = 1.0 - MUON_RATE * MUON_DECAY
    new_a = attn_w[0] * keep - MUON_RATE * 0.2 * math.sqrt(width) * take_rows(orth_a)
    scale_ff = 0.2 * math.sqrt(max(width, ff_whole))
    new_u = up_w * keep - MUON_RATE * scale_ff * take_rows(orth_u)
    new_d = down_w * keep - MUON_RATE * scale_ff * take_rows(orth_d).T
    norm_moment1 = 0.5 * norm_m1 + 0.5 * norm_grad
    norm_moment2 = 0.95 * norm_m2 + 0.05 * norm_grad * norm_grad
    first_hat = norm_moment1 / (1.0 - 0.5**STEP)
    second_hat = norm_moment2 / (1.0 - 0.95**STEP)
    norm_new = norm_params - ADAM_RATE * first_hat / (jnp.sqrt(second_hat) + 1e-08)
    return (
        mixed,
        input_grad,
        new_a[None],
        moment_a[None],
        new_u,
        moment_u,
        new_d,
        moment_d,
        norm_moment1,
        norm_moment2,
        norm_new,
    )


def solution(mesh):
    placed = (
        P(("dp", "tensor"), None),
        P(("dp", "tensor"), None),
        P("dp"),
        P("tensor", "dp", None),
        P("dp", "tensor"),
        P("tensor", "dp"),
        P(),
        P("tensor", "dp", None),
        P("dp", "tensor"),
        P("tensor", "dp"),
        P(),
        P(),
    )
    return jax.shard_map(
        on_device,
        mesh=mesh,
        in_specs=placed,
        out_specs=(
            P(("dp", "tensor"), None),
            P(("dp", "tensor"), None),
            P("tensor", "dp", None),
            P("tensor", "dp", None),
            P("dp", "tensor"),
            P("dp", "tensor"),
            P("tensor", "dp"),
            P("tensor", "dp"),
            P(),
            P(),
            P(),
        ),
        check_vma=False,
    )
```

profile of v0, /device:TPU:1, one launch (start us, length us, event | category | flops | bytes accessed | tf_op | source)
XLA Modules:
  0.0 924.6 jit_solution(2369360294010391600)
XLA Ops:
  11.0 41.7 %all-gather.15.cloned.1.call-done = bf16[1,768,768]{2,1,0:T(8,128)(2,1)} async-done(((bf16[1,96,768]{2,1,0:T(8,128)(2,1)}), bf16[1,768,768]{2,1,0:T(8,128)(2,1)}) %all-gather.15.cloned.1.call-update) | async-done | bytes 1179664 | tf_op jit(solution)/shard_map/all_gather | solution.py:198
  55.7 19.4 %all-gather.13.cloned.1.call-done = bf16[1024,768]{0,1:T(8,128)(2,1)} async-done(((bf16[256,768]{0,1:T(8,128)(2,1)}), bf16[1024,768]{0,1:T(8,128)(2,1)}) %all-gather.13.cloned.1.call-update) | async-done | bytes 1572880 | tf_op jit(solution)/shard_map/all_gather | solution.py:207
  75.2 39.1 %all-gather.17.cloned.1.call-done = bf16[4,768,768]{2,1,0:T(8,128)(2,1)} async-done(((bf16[1,768,768]{2,1,0:T(8,128)(2,1)}), bf16[4,768,768]{2,1,0:T(8,128)(2,1)}) %all-gather.17.cloned.1.call-update) | async-done | bytes 4718608 | tf_op jit(solution)/shard_map/all_gather | solution.py:202
  121.3 6.5 add_divide_fusion
  131.6 6.6 copy.193
  138.2 6.5 add_divide_fusion.1
  148.4 6.6 copy.191
  155.0 7.5 multiply_convert_fusion.2
  169.6 7.9 subtract_convert_fusion.1
  194.2 7.5 fusion.99
  205.9 5.4 convert_element_type.346
  230.8 25.9 %reduce-scatter.3.cloned.1.call-done = bf16[256,768]{0,1:T(8,128)(2,1)} async-done(((bf16[1024,768]{0,1:T(8,128)(2,1)}), bf16[256,768]{0,1:T(8,128)(2,1)}) %reduce-scatter.3.cloned.1.call-update) | async-done | bytes 393232 | tf_op jit(solution)/shard_map/reduce_scatter | solution.py:239
  262.8 20.0 %all-gather.23.cloned.1.call-done = bf16[1024,768]{0,1:T(8,128)(2,1)} async-done(((bf16[256,768]{0,1:T(8,128)(2,1)}), bf16[1024,768]{0,1:T(8,128)(2,1)}) %all-gather.23.cloned.1.call-update) | async-done | bytes 1572880 | tf_op jit(solution)/shard_map/all_gather | solution.py:254
  282.8 6.0 fusion.7
  293.2 27.2 %reduce-scatter.5.cloned.1.call-done = bf16[256,768]{0,1:T(8,128)(2,1)} async-done(((bf16[1024,768]{0,1:T(8,128)(2,1)}), bf16[256,768]{0,1:T(8,128)(2,1)}) %reduce-scatter.5.cloned.1.call-update) | async-done | bytes 393232 | tf_op jit(solution)/shard_map/reduce_scatter | solution.py:261
  334.3 5.5 all-to-all-start.1
  349.9 5.8 divide_convert_fusion
  378.5 6.5 bitcast_add_fusion
  388.8 6.6 rev.12
  395.5 7.0 fusion.101
  402.5 6.4 subtract_convert_fusion
  414.8 11.1 %fusion.96 = (f32[1024,12,64]{2,0,1:T(8,128)}, f32[1024,12,64]{2,0,1:T(8,128)}) fusion(f32[1024,12,128]{2,0,1:T(8,128)} %bitcast.203), kind=kLoop, calls=%fused_computation.224 | loop fusion | bytes 12582912 | tf_op jit(solution)/shard_map/slice | solution.py:90
  425.9 10.9 %fusion.97 = (f32[1024,12,64]{2,0,1:T(8,128)}, f32[1024,12,64]{2,0,1:T(8,128)}) fusion(f32[1024,12,128]{2,0,1:T(8,128)} %bitcast.202), kind=kLoop, calls=%fused_computation.225 | loop fusion | bytes 12582912 | tf_op jit(solution)/shard_map/slice | solution.py:90
  447.2 6.1 copy.252
  453.3 6.1 copy.253
  459.5 6.1 copy.250
  465.6 6.1 copy.251
  471.7 9.1 multiply_convert_fusion.4
  491.6 5.4 all-to-all-start
  500.0 50.6 %all-to-all-done = bf16[8,96,1536]{2,1,0:T(8,128)(2,1)} async-done(((bf16[8,96,1536]{2,1,0:T(8,128)(2,1)}), bf16[8,96,1536]{2,1,0:T(8,128)(2,1)}, u32[]{:S(2)}, u32[]{:S(2)}) %all-to-all-start) | async-done | bytes 2359328 | tf_op jit(solution)/shard_map/all_to_all | solution.py:33
  558.5 38.2 %all-reduce = (f32[6]{0:T(128)}, f32[4,768]{1,0:T(4,128)}) all-reduce(f32[6]{0:T(128)} %pad_maximum_fusion.3, f32[4,768]{1,0:T(4,128)S(1)} %pad_maximum_fusion.2), channel_id=1, replica_groups=mesh['dp'=8,'tensor'=4] {'dp','tensor'}, use_global_device_ids=true, to_apply=%region_22.23 | all-reduce | flops 3078 | bytes 24624 | tf_op jit(solution)/shard_map/psum | solution.py:308
  606.7 35.0 %all-gather.33.cloned.1.call-done = bf16[768,768]{1,0:T(8,128)(2,1)} async-done(((bf16[96,768]{1,0:T(8,128)(2,1)}), bf16[768,768]{1,0:T(8,128)(2,1)}) %all-gather.33.cloned.1.call-update) | async-done | bytes 1179664 | tf_op jit(solution)/shard_map/all_gather | solution.py:318
  641.8 42.5 %all-gather.29.cloned.1.call-done = bf16[768,768]{1,0:T(8,128)(2,1)} async-done(((bf16[96,768]{1,0:T(8,128)(2,1)}), bf16[768,768]{1,0:T(8,128)(2,1)}) %all-gather.29.cloned.1.call-update) | async-done | bytes 1179664 | tf_op jit(solution)/shard_map/all_gather | solution.py:317
  696.6 30.2 %all-gather.27.cloned.1.call-done = bf16[768,768]{1,0:T(8,128)(2,1)} async-done(((bf16[96,768]{1,0:T(8,128)(2,1)}), bf16[768,768]{1,0:T(8,128)(2,1)}) %all-gather.27.cloned.1.call-update) | async-done | bytes 1179664 | tf_op jit(solution)/shard_map/all_gather | solution.py:316
  740.7 25.6 %all-gather.35.cloned.1.call-done = bf16[768,3072]{1,0:T(8,128)(2,1)} async-done(((bf16[768,768]{1,0:T(8,128)(2,1)}), bf16[768,3072]{1,0:T(8,128)(2,1)}) %all-gather.35.cloned.1.call-update) | async-done | bytes 4718608 | tf_op jit(solution)/shard_map/all_gather | solution.py:324
  766.3 38.9 %all-gather.31.cloned.1.call-done = bf16[768,3072]{1,0:T(8,128)(2,1)} async-done(((bf16[768,768]{1,0:T(8,128)(2,1)}), bf16[768,3072]{1,0:T(8,128)(2,1)}) %all-gather.31.cloned.1.call-update) | async-done | bytes 4718608 | tf_op jit(solution)/shard_map/all_gather | solution.py:323
  805.2 8.1 fusion.23
  813.4 10.7 %add_convert_fusion.4 = bf16[768,3072]{1,0:T(8,128)(2,1)} fusion(bf16[768,3072]{1,0:T(8,128)(2,1)} %all-gather.31.cloned.1.call-done, bf16[768,3072]{1,0:T(8,128)(2,1)} %all-gather.35.cloned.1.call-done, pred[]{:T(512)S(6)} %eq.23, bf16[768,768]{1,0:T(8,128)(2,1)S(1)} %fusion.23), kind=kOutput, calls=%fused_computation.4 | convolution fusion | flops 4546953216 | bytes 15335425 | tf_op jit(solution)/shard_map/dot_general | solution.py:167
  824.1 7.6 convolution_convert_fusion.6
  831.7 10.0 %add_convert_fusion.3 = bf16[768,3072]{1,0:T(8,128)(2,1)} fusion(bf16[768,3072]{1,0:T(8,128)(2,1)} %add_convert_fusion.4, bf16[768,768]{1,0:T(8,128)(2,1)S(1)} %convolution_convert_fusion.6), kind=kOutput, calls=%fused_computation.3 | convolution fusion | flops 4542234624 | bytes 10616832 | tf_op jit(solution)/shard_map/dot_general | solution.py:167
  841.7 7.6 convolution_convert_fusion.5
  849.4 10.2 %add_convert_fusion.2 = bf16[768,3072]{1,0:T(8,128)(2,1)} fusion(bf16[768,3072]{1,0:T(8,128)(2,1)} %add_convert_fusion.3, bf16[768,768]{1,0:T(8,128)(2,1)S(1)} %convolution_convert_fusion.5), kind=kOutput, calls=%fused_computation.2 | convolution fusion | flops 4542234624 | bytes 10616832 | tf_op jit(solution)/shard_map/dot_general | solution.py:167
  859.6 7.6 convolution_convert_fusion.4
  867.2 10.0 %add_convert_fusion.1 = bf16[768,3072]{1,0:T(8,128)(2,1)} fusion(bf16[768,3072]{1,0:T(8,128)(2,1)} %add_convert_fusion.2, bf16[768,768]{1,0:T(8,128)(2,1)S(1)} %convolution_convert_fusion.4), kind=kOutput, calls=%fused_computation.1 | convolution fusion | flops 4542234624 | bytes 10616832 | tf_op jit(solution)/shard_map/dot_general | solution.py:167
  877.2 7.6 convolution_convert_fusion.3
  884.9 10.2 %add_convert_fusion = bf16[768,3072]{1,0:T(8,128)(2,1)} fusion(bf16[768,3072]{1,0:T(8,128)(2,1)} %add_convert_fusion.1, bf16[768,768]{1,0:T(8,128)(2,1)S(1)} %convolution_convert_fusion.3), kind=kOutput, calls=%fused_computation | convolution fusion | flops 4542234624 | bytes 10616832 | tf_op jit(solution)/shard_map/dot_general | solution.py:167
  896.7 6.0 add_convert_fusion.12
  906.6 6.1 fusion.31
  (270 shorter events, 211.0 us)
Async XLA Ops:
  7.2 45.6 %copy-start.22 = (f32[96,768]{1,0:T(8,128)S(1)}, f32[96,768]{1,0:T(8,128)}, u32[]{:S(2)}) copy-start(f32[96,768]{1,0:T(8,128)} %param.16) | copy-start | bytes 884740
  7.2 46.4 %copy-start.20 = (f32[768,96]{0,1:T(8,128)S(1)}, f32[768,96]{0,1:T(8,128)}, u32[]{:S(2)}) copy-start(f32[768,96]{0,1:T(8,128)} %param.17) | copy-start | bytes 884740
  7.2 47.8 %copy-start.36 = (f32[4,768]{1,0:T(4,128)S(1)}, f32[4,768]{1,0:T(4,128)}, u32[]{:S(2)}) copy-start(f32[4,768]{1,0:T(4,128)} %param.18) | copy-start | bytes 36868
  7.2 45.5 %all-gather.15.cloned.1.call-start = ((), (), s32[]{:S(2)}) async-start(), calls=%async_computation.5 | async-start | bytes 1327104 | tf_op jit(solution)/shard_map/all_gather | solution.py:198
  9.0 66.2 %all-gather.13.cloned.1.call-start = ((), (), s32[]{:S(2)}) async-start(), calls=%async_computation.4 | async-start | bytes 1966080 | tf_op jit(solution)/shard_map/all_gather | solution.py:207
  11.0 103.2 %all-gather.17.cloned.1.call-start = ((), (), s32[]{:S(2)}) async-start(), calls=%async_computation.6 | async-start | bytes 5898240 | tf_op jit(solution)/shard_map/all_gather | solution.py:202
  52.7 165.8 %all-gather.19.cloned.1.call-start = ((), (), s32[]{:S(2)}) async-start(), calls=%async_computation.7 | async-start | bytes 1327104 | tf_op jit(solution)/shard_map/all_gather | solution.py:199
  53.5 170.4 %all-gather.21.cloned.1.call-start = ((), (), s32[]{:S(2)}) async-start(), calls=%async_computation.8 | async-start | bytes 1327104 | tf_op jit(solution)/shard_map/all_gather | solution.py:200
  54.3 202.5 %reduce-scatter.3.cloned.1.call-start = ((), (), s32[]{:S(2)}) async-start(), calls=%async_computation.9 | async-start | bytes 1966080 | tf_op jit(solution)/shard_map/reduce_scatter | solution.py:239
  54.3 134.6 %copy-start.25 = (f32[64,64]{0,1:T(8,128)}, f32[64,64]{0,1:T(8,128)S(1)}, u32[]{:S(2)}) copy-start(f32[64,64]{0,1:T(8,128)S(1)} %fusion.54) | copy-start | bytes 49156
  165.7 16.5 %copy-start.27 = (f32[16,12,128]{2,1,0:T(8,128)}, f32[16,12,128]{2,1,0:T(8,128)S(1)}, u32[]{:S(2)}) copy-start(f32[16,12,128]{2,1,0:T(8,128)S(1)} %reduce-window_subtract_fusion) | copy-start | bytes 294916
  182.2 12.0 %copy-start.1 = (bf16[16,64,12,128]{3,1,2,0:T(8,128)(2,1)}, bf16[16,64,12,128]{3,1,2,0:T(8,128)(2,1)S(1)}, u32[]{:S(2)}) copy-start(bf16[16,64,12,128]{3,1,2,0:T(8,128)(2,1)S(1)} %pad_maximum_fusion) | copy-start | bytes 9437188
  187.2 7.0 copy-start.32
  194.2 7.5 copy-start.29
  228.9 53.8 %all-gather.23.cloned.1.call-start = ((), (), s32[]{:S(2)}) async-start(), calls=%async_computation.10 | async-start | bytes 1966080 | tf_op jit(solution)/shard_map/all_gather | solution.py:254
  230.1 28.0 %copy-start.38 = (f32[1024]{0:T(1024)}, f32[1024]{0:T(1024)S(1)}, u32[]{:S(2)}) copy-start(f32[1024]{0:T(1024)S(1)} %fusion.61) | copy-start | bytes 12292
  262.3 58.1 %reduce-scatter.5.cloned.1.call-start = ((), (), s32[]{:S(2)}) async-start(), calls=%async_computation.11 | async-start | bytes 1966080 | tf_op jit(solution)/shard_map/reduce_scatter | solution.py:261
  282.8 7.2 copy-start.56
  292.5 54.8 %all-gather.25.cloned.1.call-start = ((), (), s32[]{:S(2)}) async-start(), calls=%async_computation.12 | async-start | bytes 1966080 | tf_op jit(solution)/shard_map/all_gather | solution.py:273
  334.3 157.4 %all-to-all-start.1 = ((bf16[8,768,96]{1,2,0:T(8,128)(2,1)}), bf16[8,768,96]{1,2,0:T(8,128)(2,1)}, u32[]{:S(2)}, u32[]{:S(2)}) async-start(bf16[8,768,96]{1,2,0:T(8,128)(2,1)} %bitcast.217), calls=%async_computation.3 | async-start | bytes 2359296 | tf_op jit(solution)/shard_map/all_to_all | solution.py:33
  349.9 5.9 slice-start
  349.9 5.8 copy-start.18
  349.9 5.9 copy-start.33
  349.9 5.9 slice-start.1
  349.9 5.9 copy-start.26
  355.7 8.2 copy-start.7
  372.8 5.7 copy-start.28
  395.5 13.5 %slice-start.2 = ((s8[6291456]{0:T(1024)(128)(4,1)}), s8[2097152]{0:T(1024)(128)(4,1)S(1)}, s32[]{:S(2)}) async-start(s8[6291456]{0:T(1024)(128)(4,1)} %bitcast.206), calls=%async_computation.20 | async-start | bytes 4194304
  402.5 6.4 copy-start.6
  402.5 7.1 slice-start.3
  465.6 6.1 copy-start.39
  471.7 9.2 copy-start.14
  471.7 9.2 copy-start.15
  491.6 5.5 copy-start.40
  491.6 7.0 copy-start.34
  491.6 8.3 copy-start.42
  491.6 58.9 %all-to-all-start = ((bf16[8,96,1536]{2,1,0:T(8,128)(2,1)}), bf16[8,96,1536]{2,1,0:T(8,128)(2,1)}, u32[]{:S(2)}, u32[]{:S(2)}) async-start(bf16[8,96,1536]{2,1,0:T(8,128)(2,1)} %bitcast.208), calls=%async_computation.2 | async-start | bytes 4718592 | tf_op jit(solution)/shard_map/all_to_all | solution.py:33
  497.0 144.7 %all-gather.33.cloned.1.call-start = ((), (), s32[]{:S(2)}) async-start(), calls=%async_computation.16 | async-start | bytes 1327104 | tf_op jit(solution)/shard_map/all_gather | solution.py:318
  553.5 130.9 %copy-start.16 = (bf16[256,768]{0,1:T(8,128)(2,1)S(1)}, bf16[256,768]{0,1:T(8,128)(2,1)}, u32[]{:S(2)}) copy-start(bf16[256,768]{0,1:T(8,128)(2,1)} %get-tuple-element.109) | copy-start | bytes 1179652
  600.4 84.0 %all-gather.29.cloned.1.call-start = ((), (), s32[]{:S(2)}) async-start(), calls=%async_computation.14 | async-start | bytes 1327104 | tf_op jit(solution)/shard_map/all_gather | solution.py:317
  602.8 124.1 %all-gather.27.cloned.1.call-start = ((), (), s32[]{:S(2)}) async-start(), calls=%async_computation.13 | async-start | bytes 1327104 | tf_op jit(solution)/shard_map/all_gather | solution.py:316
  606.7 159.7 %all-gather.35.cloned.1.call-start = ((), (), s32[]{:S(2)}) async-start(), calls=%async_computation.17 | async-start | bytes 5898240 | tf_op jit(solution)/shard_map/all_gather | solution.py:324
  641.8 163.5 %all-gather.31.cloned.1.call-start = ((), (), s32[]{:S(2)}) async-start(), calls=%async_computation.15 | async-start | bytes 5898240 | tf_op jit(solution)/shard_map/all_gather | solution.py:323
  738.6 74.8 %copy-start.58 = (bf16[768,768]{1,0:T(8,128)(2,1)}, bf16[768,768]{1,0:T(8,128)(2,1)S(1)}, u32[]{:S(2)}) copy-start(bf16[768,768]{1,0:T(8,128)(2,1)S(1)} %add_convert_fusion.14) | copy-start | bytes 3538948
  896.4 18.1 %collective-permute-start = (bf16[768,768]{1,0:T(8,128)(2,1)S(1)}, bf16[768,768]{1,0:T(8,128)(2,1)S(1)}, u32[]{:S(2)}, u32[]{:S(2)}) collective-permute-start(bf16[768,768]{1,0:T(8,128)(2,1)S(1)} %constant_dynamic-slice_fusion), channel_id=1, source_target_pairs={{0,1},{1,0},{2,3},{3,2},{4,5},{5,4},{6,7},{7,6},{8,9},{9,8},{10,11... | collective-permute-start | bytes 3538952 | tf_op jit(solution)/shard_map/ppermute | solution.py:45
  906.6 6.1 copy-start.19
  906.6 7.9 copy-start.21
  906.6 9.6 %copy-start.23 = (f32[96,768]{1,0:T(8,128)S(1)}, f32[96,768]{1,0:T(8,128)}, u32[]{:S(2)}) copy-start(f32[96,768]{1,0:T(8,128)} %param.16) | copy-start | bytes 884740
  (33 other events, 108.6 us)
Sparse Core Ops, SparseCore 0:
  10.8 41.8 all-gather.14
  54.8 20.2 all-gather.12
  76.7 37.4 all-gather.16
  116.8 39.3 all-gather.18
  158.9 39.8 all-gather.20
  229.0 27.6 reduce-scatter.2
  262.4 20.2 all-gather.22
  292.6 27.7 reduce-scatter.4
  327.0 20.2 all-gather.24
  600.5 41.2 all-gather.32
  644.5 39.8 all-gather.28
  687.0 39.8 all-gather.26
  728.4 37.8 all-gather.34
  767.7 37.4 all-gather.30
where the time goes:
time: 936 us; the launch traced here: 925 us
  waiting for transfers between devices  399 us (43%)
  matrix products  239 us (26%)
  local copies, waits for them, and re-layouts  130 us (14%)
  other arithmetic  88 us (9%)
  blocking collectives  38.2 us (4%)
  between operations  17.9 us (2%)
  starting transfers between devices  12.1 us (1%)
    dot_general x10, matrix products, newton_update(): jnp.dot(poly, iterate, preferred_element_type=jnp.float32)  69.8 us
    all_to_all x2, waiting for transfers between devices, sum_at_owner(): pieces = lax.all_to_all(cut_along(array, dim, size), axis, 0, 0, tiled=True)  50.6 us
    dot_general x10, matrix products, orthogonalize(): jnp.dot(iterate, iterate.T, preferred_element_type=jnp.float32)  49.8 us
    all_gather x1, waiting for transfers between devices, on_device(): lax.all_gather(start_u, 'dp', axis=0, tiled=True)  42.5 us
    all_gather x1, waiting for transfers between devices, on_device(): lax.all_gather(attn_w.astype(jnp.bfloat16), 'dp', axis=1, tiled=True)  41.7 us
    all_gather x1, waiting for transfers between devices, on_device(): w_all = lax.all_gather(wa_rows, 'tensor', axis=0, tiled=True)  39.1 us
    all_gather x1, waiting for transfers between devices, on_device(): lax.all_gather(cols_u, 'tensor', axis=1, tiled=True)  38.9 us
    psum x1, blocking collectives, on_device(): totals, norm_grad = lax.psum((squares, norm_partial), ('dp', 'tensor'))  38.2 us
  transfers between devices with their start and end apart: 17, of which 13 were waited for; matrix products, arithmetic and copies ran while one was open for 35% of the time, Pallas kernels for 0%

commit v1 on v0

--- a/solution.py
+++ b/solution.py
@@ -1,8 +1,12 @@
+import functools
 import math
+import types
 
 import jax
 import jax.numpy as jnp
 from jax import lax
+from jax.experimental import pallas as pl
+from jax.experimental.pallas import tpu as pltpu
 from jax.sharding import PartitionSpec as P
 
 HEADS = 12
@@ -363,6 +367,1208 @@
     )
 
 
+BF = jnp.bfloat16
+F32 = jnp.float32
+MESH = pl.DeviceIdType.MESH
+TENSOR = 4
+QUARTER = 256
+LANES = 128
+VMEM_LIMIT = 62 << 20
+GELU_C = math.sqrt(2.0 / math.pi)
+GELU_A = 0.044715
+
+
+def nn(left, right):
+    return jnp.dot(left, right, preferred_element_type=F32)
+
+
+def nt(left, right):
+    return lax.dot_general(left, right, (((1,), (1,)), ((), ())), preferred_element_type=F32)
+
+
+def tn(left, right):
+    return lax.dot_general(left, right, (((0,), (0,)), ((), ())), preferred_element_type=F32)
+
+
+def lanes_of(rows, cols=LANES):
+    return lax.broadcasted_iota(jnp.int32, (rows, cols), 1)
+
+
+def half_roll(array):
+    return pltpu.roll(array, LANES // 2, 1)
+
+
+def place():
+    data = lax.axis_index("dp")
+    tensor = lax.axis_index("tensor")
+    return data, tensor
+
+
+def greet(devices):
+    barrier = pltpu.get_barrier_semaphore()
+    for device in devices:
+        pl.semaphore_signal(barrier, inc=1, device_id=device, device_id_type=MESH)
+    pl.semaphore_wait(barrier, len(devices))
+
+
+def send(src, dst, send_sem, recv_sem, device):
+    copy = pltpu.make_async_remote_copy(
+        src_ref=src,
+        dst_ref=dst,
+        send_sem=send_sem,
+        recv_sem=recv_sem,
+        device_id=device,
+        device_id_type=MESH,
+    )
+    copy.start()
+    return copy
+
+
+def kernel_call(body, name, ins, outs, scratch, collective):
+    in_names = list(ins)
+    out_names = list(outs)
+    scratch_names = list(scratch)
+
+    def kernel(*refs):
+        body(types.SimpleNamespace(**dict(zip(in_names + out_names + scratch_names, refs))))
+
+    results = pl.pallas_call(
+        kernel,
+        name=name,
+        out_shape=[outs[n] for n in out_names],
+        in_specs=[pl.BlockSpec(memory_space=pltpu.VMEM)] * len(in_names),
+        out_specs=[pl.BlockSpec(memory_space=pltpu.VMEM)] * len(out_names),
+        scratch_shapes=[scratch[n] for n in scratch_names],
+        compiler_params=pltpu.CompilerParams(
+            collective_id=collective, has_side_effects=True, vmem_limit_bytes=VMEM_LIMIT
+        ),
+    )(*[ins[n] for n in in_names])
+    return dict(zip(out_names, results))
+
+
+def shape(*dims, dtype=BF):
+    return jax.ShapeDtypeStruct(dims, dtype)
+
+
+def dma(*dims):
+    return pltpu.SemaphoreType.DMA(dims)
+
+
+class GatherDp:
+    def __init__(self, slot_of, sends, recvs, data, tensor, count):
+        self.slot_of, self.sends, self.recvs = slot_of, sends, recvs
+        self.data, self.tensor = data, tensor
+        self.high_count = count // 2
+        self.high, self.low = data // 2, data % 2
+        self.partner = (self.high * 2 + 1 - self.low, tensor)
+        self.copies = []
+
+    def peer(self, step):
+        return lax.rem(self.high + step, self.high_count) * 2 + self.low
+
+    def start(self):
+        mine = self.slot_of(self.data)
+        n = self.high_count
+        self.along = []
+        for step in range(1, n):
+            self.along.append(
+                send(mine, mine, self.sends.at[step], self.recvs.at[step], (self.peer(step), self.tensor))
+            )
+        self.across = [send(mine, mine, self.sends.at[0], self.recvs.at[0], self.partner)]
+
+    def forward(self):
+        n = self.high_count
+        for step in range(1, n):
+            self.along[step - 1].wait_recv()
+            slot = self.slot_of(self.peer(n - step))
+            self.across.append(
+                send(slot, slot, self.sends.at[n - 1 + step], self.recvs.at[n - 1 + step], self.partner)
+            )
+
+    def finish(self):
+        for copy in self.across:
+            copy.wait_recv()
+        for copy in self.along + self.across:
+            copy.wait_send()
+
+
+def gather_body(count, r):
+    data, tensor = place()
+    core = tensor % 2
+    high, low = data // 2, data % 2
+    n = count // 2
+    group = [(data, tensor ^ k) for k in (1, 2, 3)]
+    along = [(lax.rem(high + k, n) * 2 + low, tensor) for k in range(1, n)]
+    greet(group + along + [(high * 2 + 1 - low, tensor)])
+
+    r.seq[tensor] = r.tokens[...]
+    mine = r.seq.at[tensor]
+    tok_core = send(mine, mine, r.tok_s.at[0], r.tok_r.at[0], group[0])
+    tok_x = send(mine, mine, r.tok_s.at[1], r.tok_r.at[1], group[1])
+
+    for k in (1, 2, 3):
+        peer = tensor ^ k
+
+        @pl.when(tensor < 3)
+        def _():
+            send(r.slabs.at[peer], r.wqkv.at[data, tensor], r.slab_s.at[k], r.slab_r.at[tensor], group[k - 1])
+
+        @pl.when(tensor == 3)
+        def _():
+            send(r.halves.at[peer % 2], r.wo.at[data, peer % 2], r.slab_s.at[k], r.slab_r.at[3], group[k - 1])
+
+    @pl.when(tensor < 3)
+    def _():
+        r.wqkv[data, tensor] = r.slabs[tensor]
+
+    @pl.when(tensor == 3)
+    def _():
+        r.wo[data, core] = r.halves[core]
+
+    for m in range(3):
+
+        @pl.when(tensor != m)
+        def _():
+            pltpu.make_async_copy(r.wqkv.at[data, m], r.wqkv.at[data, m], r.slab_r.at[m]).wait()
+
+    @pl.when(tensor != 3)
+    def _():
+        pltpu.make_async_copy(r.wo.at[data, core], r.wo.at[data, core], r.slab_r.at[3]).wait()
+
+    r.wu[data] = r.up[...]
+    r.wd[data] = r.down[...]
+    gathers = [
+        GatherDp(lambda d: r.wqkv.at[d], r.q_s, r.q_r, data, tensor, count),
+        GatherDp(lambda d: r.wo.at[d, core], r.o_s, r.o_r, data, tensor, count),
+        GatherDp(lambda d: r.wu.at[d], r.u_s, r.u_r, data, tensor, count),
+        GatherDp(lambda d: r.wd.at[d], r.d_s, r.d_r, data, tensor, count),
+    ]
+    for g in gathers:
+        g.start()
+    tok_x.wait_recv()
+    far = r.seq.at[tensor ^ 2]
+    tok_f = send(far, far, r.tok_s.at[2], r.tok_r.at[2], group[0])
+    for g in gathers:
+        g.forward()
+    for g in gathers:
+        g.finish()
+    share = []
+    for d in range(count):
+        part = r.wo.at[d, core]
+        share.append(send(part, part, r.share_s.at[d], r.share_r.at[d], group[0]))
+    for copy in share:
+        copy.wait_send()
+    for d in range(count):
+        part = r.wo.at[d, 1 - core]
+        pltpu.make_async_copy(part, part, r.share_r.at[d]).wait()
+    tok_core.wait_recv()
+    tok_f.wait_recv()
+    for copy in (tok_core, tok_x, tok_f):
+        copy.wait_send()
+    for k in (1, 2, 3):
+
+        @pl.when(tensor < 3)
+        def _():
+            pltpu.make_async_copy(r.slabs.at[0], r.slabs.at[0], r.slab_s.at[k]).wait()
+
+        @pl.when(tensor == 3)
+        def _():
+            pltpu.make_async_copy(r.halves.at[0], r.halves.at[0], r.slab_s.at[k]).wait()
+
+
+def gather_inputs(count, rows, tokens, slabs, halves, up, down):
+    gather_sems = {}
+    for key in "qoud":
+        gather_sems[key + "_s"] = dma(count)
+        gather_sems[key + "_r"] = dma(count)
+    return kernel_call(
+        functools.partial(gather_body, count),
+        "gather_inputs",
+        dict(tokens=tokens, slabs=slabs, halves=halves, up=up, down=down),
+        dict(
+            seq=shape(TENSOR, QUARTER, 768),
+            wqkv=shape(count, 3, rows, 256),
+            wo=shape(count, 2, rows // 2, 768),
+            wu=shape(count, rows, 768),
+            wd=shape(count, rows, 768),
+        ),
+        dict(
+            tok_s=dma(3),
+            tok_r=dma(3),
+            slab_s=dma(4),
+            slab_r=dma(4),
+            share_s=dma(count),
+            share_r=dma(count),
+            **gather_sems,
+        ),
+        0,
+    )
+
+
+def softplus_and_slope(x):
+    small = jnp.exp(-jnp.abs(x))
+    soft = jnp.maximum(x, 0.0) + jnp.log1p(small)
+    slope = jnp.where(x >= 0.0, 1.0, small) / (1.0 + small)
+    return soft, slope
+
+
+def spread_weights(r):
+    low = lanes_of(768) < 64
+    for m in range(3):
+        w = r.wqkv[:, m].reshape(768, 256)
+        first, second = w[:, :LANES].astype(F32), w[:, LANES:].astype(F32)
+        turned = half_roll(first)
+        if m < 2:
+            parts = [
+                jnp.where(low, first, turned),
+                jnp.where(low, turned, first),
+                jnp.where(low, second, half_roll(second)),
+            ]
+        else:
+            parts = [jnp.where(low, p, 0.0) for p in (first, turned, second)]
+        for h, part in enumerate(parts):
+            r.wall[:, (3 * m + h) * LANES : (3 * m + h + 1) * LANES] = part.astype(BF)
+
+
+def project(r):
+    lane = lanes_of(QUARTER)
+
+    def step(q, carry):
+        both = nn(r.seq[q], r.wall[...])
+        table, table_live = r.table[q], r.table_live[q]
+        for h in range(3):
+            soft, slope = softplus_and_slope(both[:, h * LANES : (h + 1) * LANES])
+            r.qf[h, q] = (soft * table).astype(BF)
+            r.qg[h, q] = slope * table
+            soft, slope = softplus_and_slope(both[:, (3 + h) * LANES : (4 + h) * LANES])
+            r.kf[h, q] = (soft * table_live).astype(BF)
+            r.kg[h, q] = slope * table_live
+            value = both[:, (6 + h) * LANES : (7 + h) * LANES]
+            ones = jnp.where((lane == 64) | (lane == 65), 1.0, 0.0)
+            r.va[h, q] = jnp.where(lane < 64, value, ones).astype(BF)
+        return carry
+
+    lax.fori_loop(0, TENSOR, step, 0)
+
+
+def attend(r, q):
+    lane = lanes_of(QUARTER)
+    keep = lanes_of(QUARTER, QUARTER) <= lax.broadcasted_iota(jnp.int32, (QUARTER, QUARTER), 0)
+
+    def head(h, carry):
+        qf, kf, va = r.qf[h, q], r.kf[h, q], r.va[h, q]
+        scores = jnp.where(keep, nt(qf, kf), 0.0).astype(BF)
+        r.sb[h, q] = scores
+        total = nn(scores, va)
+        if q > 0:
+            state = r.state[h].astype(BF)
+            r.st[h, q] = state
+            total = total + nn(qf, state)
+        if q < TENSOR - 1:
+            pairs = tn(kf, va)
+            r.state[h] = pairs if q == 0 else r.state[h] + pairs
+        inverse = 1.0 / total[:, 64:65]
+        r.af[h, q] = jnp.where(lane < 64, total * inverse, inverse)
+        return carry
+
+    lax.fori_loop(0, 3, head, 0)
+    zero, one, two = r.af[0, q], r.af[1, q], r.af[2, q]
+    r.attn[q, :, :LANES] = jnp.where(lane < 64, zero, half_roll(one)).astype(BF)
+    r.attn[q, :, LANES:] = jnp.where(lane < 64, two, 0.0).astype(BF)
+
+
+def norm_rows(resid):
+    center = resid - jnp.mean(resid, -1, keepdims=True)
+    spread = jnp.mean(center * center, -1, keepdims=True)
+    scale = lax.rsqrt(spread + NORM_EPS)
+    return center * scale, scale
+
+
+def norm_rows_back(normal, scale, grad):
+    return scale * (
+        grad
+        - jnp.mean(grad, -1, keepdims=True)
+        - normal * jnp.mean(grad * normal, -1, keepdims=True)
+    )
+
+
+class Group:
+    def __init__(self):
+        self.data, self.tensor = place()
+        self.far, self.core = self.tensor // 2, self.tensor % 2
+
+    def device(self, k):
+        return (self.data, self.tensor ^ k)
+
+
+def spread_quarter(r, g, buf, sends, recvs):
+    own = buf.at[g.tensor]
+    far = send(own, own, sends.at[0], recvs.at[0], g.device(2))
+    near = send(own, own, sends.at[1], recvs.at[1], g.device(1))
+
+    def arrived_near():
+        near.wait_recv()
+
+    def arrived_far():
+        far.wait_recv()
+        slot = buf.at[g.tensor ^ 2]
+        passed = send(slot, slot, sends.at[2], recvs.at[2], g.device(1))
+        passed.wait_recv()
+        for copy in (far, near, passed):
+            copy.wait_send()
+
+    return arrived_near, arrived_far
+
+
+class SumQuarters:
+    def __init__(self, r, g, slot):
+        self.r, self.g, self.slot = r, g, slot
+
+    def near_out(self, j, value):
+        r, k = self.r, self.slot * 2 + j
+        r.near_send[k] = value.astype(BF)
+        self.copy = send(r.near_send.at[k], r.near_recv.at[k], r.near_s.at[k], r.near_r.at[k], self.g.device(1))
+        self.copies = getattr(self, "copies", []) + [self.copy]
+
+    def near_in(self, j, value):
+        self.copies[j].wait_recv()
+        return value + self.r.near_recv[self.slot * 2 + j].astype(F32)
+
+    def far_out(self, value):
+        r, k = self.r, self.slot
+        r.far_send[k] = value.astype(BF)
+        self.far = send(r.far_send.at[k], r.far_recv.at[k], r.far_s.at[k], r.far_r.at[k], self.g.device(2))
+
+    def far_in(self, value):
+        self.far.wait_recv()
+        value = value + self.r.far_recv[self.slot].astype(F32)
+        for copy in self.copies + [self.far]:
+            copy.wait_send()
+        return value
+
+
+def feed(r, q):
+    pre = nn(r.hb[q], r.wu[...].reshape(768, 768))
+    inner = jnp.tanh(GELU_C * (pre + GELU_A * pre * pre * pre))
+    half = 0.5 * (1.0 + inner)
+    r.gp[q] = half + 0.5 * pre * (1.0 - inner * inner) * (GELU_C * (1.0 + 3.0 * GELU_A * pre * pre))
+    hid = (pre * half).astype(BF)
+    r.hid[q] = hid
+    return nt(hid, r.wd[...].reshape(768, 768))
+
+
+def feed_back(r, q):
+    grad_act = nn(r.dr2[q], r.wd[...].reshape(768, 768))
+    grad_pre = (grad_act * r.gp[q]).astype(BF)
+    r.du[q] = grad_pre
+    return nt(grad_pre, r.wu[...].reshape(768, 768))
+
+
+def attend_back(r, g, q):
+    lane = lanes_of(QUARTER)
+    keep = lanes_of(QUARTER, QUARTER) <= lax.broadcasted_iota(jnp.int32, (QUARTER, QUARTER), 0)
+    dr1 = r.dr1[q]
+
+    def head(h, carry):
+        grad = nt(dr1, r.woh[h])
+        af = r.af[h, q]
+        inverse = af[:, 64:65]
+        dden = -jnp.sum(grad * af, -1, keepdims=True) * inverse
+        dden_low = dden.astype(BF).astype(F32)
+        extra = jnp.where(lane == 64, dden_low, jnp.where(lane == 65, dden - dden_low, 0.0))
+        dnum = jnp.where(lane < 64, grad * inverse, extra).astype(BF)
+        qf, kf, va, sb = r.qf[h, q], r.kf[h, q], r.va[h, q], r.sb[h, q]
+        ds = jnp.where(keep, nt(dnum, va), 0.0).astype(BF)
+        dqf = nn(ds, kf)
+        if q > 0:
+            dqf = dqf + nt(dnum, r.st[h, q])
+        dkf = tn(ds, qf)
+        dv = tn(sb, dnum)
+        if q < TENSOR - 1:
+            dkv = r.state[h].astype(BF)
+            dkf = dkf + nt(va, dkv)
+            dv = dv + nn(kf, dkv)
+        if q > 0:
+            pairs = tn(qf, dnum)
+            r.state[h] = pairs if q == TENSOR - 1 else r.state[h] + pairs
+        dqf = dqf * r.qg[h, q]
+        dkf = dkf * r.kg[h, q]
+        r.fold[0, h] = dqf + half_roll(dqf)
+        r.fold[1, h] = dkf + half_roll(dkf)
+        r.fold[2, h] = dv
+        return carry
+
+    lax.fori_loop(0, 3, head, 0)
+    for m in range(3):
+        second = r.fold[m, 1] if m < 2 else half_roll(r.fold[m, 1])
+        r.dqkv[q, :, 256 * m : 256 * m + LANES] = jnp.where(lane < 64, r.fold[m, 0], second).astype(BF)
+        r.dqkv[q, :, 256 * m + LANES : 256 * (m + 1)] = jnp.where(lane < 64, r.fold[m, 2], 0.0).astype(BF)
+    total = None
+    for m in range(3):
+        part = nt(r.dqkv[q, :, 256 * m : 256 * (m + 1)], r.wqkv[:, m].reshape(768, 256))
+        total = part if total is None else total + part
+    r.ig[q] = total
+
+
+def layer_body(r):
+    g = Group()
+    tensor, far, core = g.tensor, g.far, g.core
+    greet([g.device(k) for k in (1, 2, 3)])
+    spread_weights(r)
+    for t in range(TENSOR):
+        r.wop[t, :192] = r.wo[192 * t : 192 * (t + 1)]
+        r.wop[t, 192:] = jnp.zeros((64, 768), BF)
+    for h in range(3):
+        r.woh[h, :64] = r.wo[pl.ds(pl.multiple_of(192 * tensor + 64 * h, 64), 64)]
+        r.woh[h, 64:] = jnp.zeros((64, 768), BF)
+    project(r)
+
+    copies = [[], []]
+    for j in range(2):
+        attend(r, 2 * j)
+        attend(r, 2 * j + 1)
+        mine, other = 2 * j + core, 2 * j + 1 - core
+        for k in (2, 1, 3):
+            quarter = mine if k == 2 else other
+            copies[j].append(
+                send(r.attn.at[quarter], r.aall.at[tensor, j], r.attn_s.at[j, k], r.attn_r.at[j, k], g.device(k))
+            )
+        r.aall[tensor, j] = r.attn[mine]
+
+    gain1, bias1, gain2, bias2 = (r.norms[k : k + 1] for k in range(4))
+    hs = []
+    for own in (False, True):
+        j = far if own else 1 - far
+        for copy in copies[1] if False else []:
+            copy.wait_recv()
+        if not own:
+            for group_copies in copies:
+                for copy in group_copies:
+                    copy.wait_recv()
+        q = 2 * j + core
+        branch = nn(r.aall[0, j], r.wop[0])
+        for t in range(1, TENSOR):
+            branch = branch + nn(r.aall[t, j], r.wop[t])
+        normal, scale = norm_rows(r.seq[q].astype(F32) + branch)
+        hidden = normal * gain1 + bias1
+        r.hb[q] = hidden.astype(BF)
+        if own:
+            r.n1[...] = normal
+            r.s1[...] = jnp.broadcast_to(scale, (QUARTER, LANES))
+            r.h1[...] = hidden
+        hs.append(send(r.hb.at[q], r.hb.at[q], r.h_s.at[int(own)], r.h_r.at[int(own)], g.device(1)))
+    for group_copies in copies:
+        for copy in group_copies:
+            copy.wait_send()
+
+    total = SumQuarters(r, g, 0)
+    kept = feed(r, tensor ^ 2)
+    hs[0].wait_recv()
+    total.near_out(0, feed(r, tensor ^ 3))
+    kept = total.near_in(0, kept)
+    total.far_out(kept)
+    hs[1].wait_recv()
+    total.near_out(1, feed(r, tensor ^ 1))
+    kept = feed(r, tensor)
+    kept = total.far_in(total.near_in(1, kept))
+    for copy in hs:
+        copy.wait_send()
+
+    n2, s2 = norm_rows(r.h1[...] + kept)
+    live = r.live[...]
+    r.mixed[...] = (live * (n2 * gain2 + bias2)).astype(BF)
+    dy = live * r.cotangent[...].astype(F32)
+    r.partial[2:3] = jnp.sum(dy * n2, 0, keepdims=True)
+    r.partial[3:4] = jnp.sum(dy, 0, keepdims=True)
+    dr2 = norm_rows_back(n2, s2, dy * gain2)
+    r.dr2f[...] = dr2
+    r.dr2[tensor] = dr2.astype(BF)
+    near, distant = spread_quarter(r, g, r.dr2, r.dr2_s, r.dr2_r)
+
+    total = SumQuarters(r, g, 1)
+    kept_own = feed_back(r, tensor)
+    near()
+    total.near_out(0, feed_back(r, tensor ^ 1))
+    distant()
+    total.near_out(1, feed_back(r, tensor ^ 3))
+    kept = feed_back(r, tensor ^ 2)
+    total.far_out(total.near_in(1, kept))
+    kept_own = total.near_in(0, kept_own)
+    r.dh[...] = kept_own
+    grad = tn(r.hb[...].reshape(1024, 768), r.du[...].reshape(1024, 768))
+    r.gu[...] = grad.astype(BF).reshape(r.gu.shape)
+    grad = tn(r.dr2[...].reshape(1024, 768), r.hid[...].reshape(1024, 768))
+    r.gd[...] = grad.astype(BF).reshape(r.gd.shape)
+    dh = total.far_in(r.dh[...]) + r.dr2f[...]
+
+    n1 = r.n1[...]
+    r.partial[0:1] = jnp.sum(dh * n1, 0, keepdims=True)
+    r.partial[1:2] = jnp.sum(dh, 0, keepdims=True)
+    dr1 = norm_rows_back(n1, r.s1[:, :1], dh * gain1)
+    r.dr1f[...] = dr1
+    r.dr1[tensor] = dr1.astype(BF)
+    near, distant = spread_quarter(r, g, r.dr1, r.dr1_s, r.dr1_r)
+    near()
+    distant()
+
+    for q in (3, 2, 1, 0):
+        attend_back(r, g, q)
+    total = SumQuarters(r, g, 2)
+    total.near_out(0, r.ig[tensor ^ 3])
+    total.near_out(1, r.ig[tensor ^ 1])
+    total.far_out(total.near_in(0, r.ig[tensor ^ 2]))
+    grad = tn(r.seq[...].reshape(1024, 768), r.dqkv[...].reshape(1024, 768)).astype(BF)
+    for m in range(3):
+        r.ga[:, m] = grad[:, 256 * m : 256 * (m + 1)].reshape(r.ga.shape[0], r.ga.shape[2], 256)
+    grad = tn(r.attn[...].reshape(1024, 256), r.dr1[...].reshape(1024, 768)).astype(BF)
+    r.go[...] = grad[:192].reshape(r.go.shape)
+    r.input_grad[...] = total.far_in(total.near_in(1, r.ig[tensor])) + r.dr1f[...]
+
+
+def layer(count, rows, gathered, wo, cotangent, norms, live, table, table_live):
+    v = pltpu.VMEM
+    return kernel_call(
+        layer_body,
+        "layer",
+        dict(
+            seq=gathered["seq"],
+            wqkv=gathered["wqkv"],
+            wo=wo,
+            wu=gathered["wu"],
+            wd=gathered["wd"],
+            cotangent=cotangent,
+            norms=norms,
+            live=live,
+            table=table,
+            table_live=table_live,
+        ),
+        dict(
+            mixed=shape(QUARTER, 768),
+            input_grad=shape(QUARTER, 768, dtype=F32),
+            gu=shape(count, rows, 768),
+            gd=shape(count, rows, 768),
+            ga=shape(count, 3, rows, 256),
+            go=shape(2, rows, 768),
+            partial=shape(4, 768, dtype=F32),
+        ),
+        dict(
+            wall=v((768, 9 * LANES), BF),
+            wop=v((TENSOR, 256, 768), BF),
+            woh=v((3, LANES, 768), BF),
+            qf=v((3, TENSOR, QUARTER, LANES), BF),
+            kf=v((3, TENSOR, QUARTER, LANES), BF),
+            va=v((3, TENSOR, QUARTER, LANES), BF),
+            qg=v((3, TENSOR, QUARTER, LANES), F32),
+            kg=v((3, TENSOR, QUARTER, LANES), F32),
+            af=v((3, TENSOR, QUARTER, LANES), F32),
+            sb=v((3, TENSOR, QUARTER, QUARTER), BF),
+            st=v((3, TENSOR, LANES, LANES), BF),
+            state=v((3, LANES, LANES), F32),
+            attn=v((TENSOR, QUARTER, 256), BF),
+            aall=v((TENSOR, 2, QUARTER, 256), BF),
+            hb=v((TENSOR, QUARTER, 768), BF),
+            n1=v((QUARTER, 768), F32),
+            s1=v((QUARTER, LANES), F32),
+            h1=v((QUARTER, 768), F32),
+            hid=v((TENSOR, QUARTER, 768), BF),
+            gp=v((TENSOR, QUARTER, 768), F32),
+            du=v((TENSOR, QUARTER, 768), BF),
+            dr2=v((TENSOR, QUARTER, 768), BF),
+            dr2f=v((QUARTER, 768), F32),
+            dr1=v((TENSOR, QUARTER, 768), BF),
+            dr1f=v((QUARTER, 768), F32),
+            dh=v((QUARTER, 768), F32),
+            fold=v((3, 3, QUARTER, LANES), F32),
+            dqkv=v((TENSOR, QUARTER, 768), BF),
+            ig=v((TENSOR, QUARTER, 768), F32),
+            near_send=v((6, QUARTER, 768), BF),
+            near_recv=v((6, QUARTER, 768), BF),
+            far_send=v((3, QUARTER, 768), BF),
+            far_recv=v((3, QUARTER, 768), BF),
+            near_s=dma(6),
+            near_r=dma(6),
+            far_s=dma(3),
+            far_r=dma(3),
+            attn_s=dma(2, 4),
+            attn_r=dma(2, 4),
+            h_s=dma(2),
+            h_r=dma(2),
+            dr2_s=dma(3),
+            dr2_r=dma(3),
+            dr1_s=dma(3),
+            dr1_r=dma(3),
+        ),
+        1,
+    )
+
+
+def await_bytes(ref, sem):
+    pltpu.make_async_copy(ref, ref, sem).wait()
+
+
+class ReduceDp:
+    def __init__(self, src, low_buf, high_send, high_buf, sems, data, tensor, count):
+        self.src, self.low_buf, self.high_send, self.high_buf = src, low_buf, high_send, high_buf
+        self.low_s, self.low_r, self.high_s, self.high_r = sems
+        self.tensor, self.n = tensor, count // 2
+        self.high, self.low = data // 2, data % 2
+
+    def at(self, step):
+        return lax.rem(self.high + step, self.n)
+
+    def start(self):
+        partner = (self.high * 2 + 1 - self.low, self.tensor)
+        self.across = {}
+        for step in list(range(1, self.n)) + [0]:
+            h = self.at(step)
+            self.across[step] = send(
+                self.src.at[h * 2 + 1 - self.low],
+                self.low_buf.at[h],
+                self.low_s.at[step],
+                self.low_r.at[step],
+                partner,
+            )
+
+    def pair(self, step):
+        self.across[step].wait_recv()
+        h = self.at(step)
+        return self.src[h * 2 + self.low].astype(F32) + self.low_buf[h].astype(F32)
+
+    def forward(self):
+        self.along = []
+        for step in range(1, self.n):
+            self.high_send[step] = self.pair(step).astype(BF)
+            self.along.append(
+                send(
+                    self.high_send.at[step],
+                    self.high_buf.at[step],
+                    self.high_s.at[step],
+                    self.high_r.at[step],
+                    (self.at(step) * 2 + self.low, self.tensor),
+                )
+            )
+
+    def finish(self):
+        total = self.pair(0)
+        for step in range(1, self.n):
+            self.along[step - 1].wait_recv()
+            total = total + self.high_buf[step].astype(F32)
+        for copy in list(self.across.values()) + self.along:
+            copy.wait_send()
+        return total
+
+
+def assemble(r, core_rows):
+    low = lanes_of(core_rows) < 64
+    for pair in range(2):
+        even, odd = r.abuf[2 * pair].astype(F32), r.abuf[2 * pair + 1].astype(F32)
+        turned = half_roll(odd[:, :LANES])
+        base = 3 * LANES * pair
+        r.grad_a[:, base : base + LANES] = even[:, :LANES]
+        r.grad_a[:, base + LANES : base + 2 * LANES] = jnp.where(low, even[:, LANES:], turned)
+        r.grad_a[:, base + 2 * LANES : base + 3 * LANES] = jnp.where(low, turned, half_roll(odd[:, LANES:]))
+
+
+def sum_partials(r, data, tensor, count):
+    r.pbuf[tensor] = r.partial[...]
+    copies = []
+    for k in (1, 2, 3):
+        copies.append(send(r.partial, r.pbuf.at[tensor], r.pt_s.at[k], r.pt_r.at[k], (data, tensor ^ k)))
+    for copy in copies:
+        copy.wait()
+    r.psum[...] = ((r.pbuf[0] + r.pbuf[1]) + r.pbuf[2]) + r.pbuf[3]
+    r.qbuf[data] = r.psum[...]
+    copies = []
+    for k in range(1, count):
+        copies.append(
+            send(r.psum, r.qbuf.at[data], r.pd_s.at[k], r.pd_r.at[k], (lax.rem(data + k, count), tensor))
+        )
+
+    def finish():
+        for copy in copies:
+            copy.wait()
+        total = r.qbuf[0]
+        for d in range(1, count):
+            total = total + r.qbuf[d]
+        r.norm_grad[...] = total
+
+    return finish
+
+
+def reduce_body(count, rows, r):
+    data, tensor = place()
+    far, core = tensor // 2, tensor % 2
+    high, low = data // 2, data % 2
+    other = high * 2 + 1 - low
+    n = count // 2
+    greet(
+        [(data, tensor ^ k) for k in (1, 2, 3)]
+        + [(lax.rem(data + k, count), tensor) for k in range(1, count)]
+        + [(other, tensor ^ 1)]
+    )
+    finish_partials = sum_partials(r, data, tensor, count)
+    sums = {}
+    for key in "dua":
+        sums[key] = ReduceDp(
+            *(getattr(r, name + key) for name in ("g", "low", "hs", "hb")),
+            [getattr(r, name + key) for name in ("ls_", "lr_", "hs_", "hr_")],
+            data,
+            tensor,
+            count,
+        )
+    for key in "dua":
+        sums[key].start()
+    out_low = send(r.go.at[1 - low], r.olow, r.o_s.at[0], r.o_r.at[0], (other, tensor))
+    for key in "dua":
+        sums[key].forward()
+
+    out_low.wait_recv()
+    out_part = r.go[low].astype(F32) + r.olow[...].astype(F32)
+    r.osend[...] = out_part.astype(BF)
+    for k in range(1, n):
+
+        @pl.when(lax.rem(high + k, n) == tensor)
+        def _():
+            send(r.osend, r.ohigh.at[k], r.o_s.at[1], r.o_r.at[k], (tensor * 2 + low, tensor))
+
+    wide = 768
+    here = pl.ds(pl.multiple_of(data * rows, rows), rows)
+
+    def cols(t):
+        return pl.ds(pl.multiple_of(t * wide, wide), wide)
+
+    moment = 0.5 * r.down_mom[...] + sums["d"].finish()
+    r.mom_d[...] = moment
+    r.xsd[...] = moment.astype(BF)
+    moment = 0.5 * r.up_mom[...] + sums["u"].finish()
+    r.mom_u[...] = moment
+    r.xsu[...] = moment.astype(BF)
+    own = r.xmat.at[here, cols(tensor)]
+    mine = r.xmat.at[here, cols(tensor ^ 2)]
+
+    @pl.when(far == 0)
+    def _():
+        r.xmat[here, cols(tensor)] = r.xsu[...]
+        send(r.xsd, own, r.swap_s, r.swap_r, (data, tensor ^ 2))
+
+    @pl.when(far == 1)
+    def _():
+        r.xmat[here, cols(tensor)] = r.xsd[...]
+        send(r.xsu, own, r.swap_s, r.swap_r, (data, tensor ^ 2))
+
+    gathers = [
+        GatherDp(lambda d: r.xmat.at[pl.ds(pl.multiple_of(d * rows, rows), rows), cols(tensor)], r.x_s, r.x_r, data, tensor, count),
+        GatherDp(lambda d: r.xmat.at[pl.ds(pl.multiple_of(d * rows, rows), rows), cols(tensor ^ 2)], r.y_s, r.y_r, data, tensor, count),
+    ]
+    gathers[0].start()
+    await_bytes(mine, r.swap_r)
+    gathers[1].start()
+
+    total = sums["a"].finish()
+    for m in range(3):
+        r.asend[m] = total[m].astype(BF)
+    for m in range(3):
+
+        @pl.when(tensor != m)
+        def _():
+            send(r.asend.at[m], r.abuf.at[tensor], r.a_s.at[m], r.a_r.at[tensor], (data, m))
+
+        @pl.when(tensor == m)
+        def _():
+            r.abuf[tensor] = r.asend[m]
+
+    for k in range(1, n):
+
+        @pl.when(high == tensor)
+        def _():
+            await_bytes(r.ohigh.at[k], r.o_r.at[k])
+
+    @pl.when(high == tensor)
+    def _():
+        whole = out_part
+        for k in range(1, n):
+            whole = whole + r.ohigh[k].astype(F32)
+        r.grad_a[...] = whole
+        r.oout[...] = whole.astype(BF)
+
+    @pl.when((high == tensor) & (tensor != 3))
+    def _():
+        send(r.oout, r.oin, r.o_s.at[2], r.oin_r, (data, 3))
+
+    @pl.when((tensor == 3) & (high != 3))
+    def _():
+        await_bytes(r.oin, r.oin_r)
+        r.grad_a[...] = r.oin[...].astype(F32)
+
+    for t in range(TENSOR):
+
+        @pl.when((tensor < 3) & (tensor != t))
+        def _():
+            await_bytes(r.abuf.at[t], r.a_r.at[t])
+
+    @pl.when(tensor < 3)
+    def _():
+        assemble(r, rows)
+
+    moment = 0.5 * r.attn_mom[...] + r.grad_a[...]
+    r.mom_a[...] = moment
+    r.xsa[...] = moment.astype(BF)
+
+    slot = r.xa.at[here]
+    there = (high * 2 + core, far * 2 + 1)
+
+    @pl.when((core == 1) & (low == 1))
+    def _():
+        r.xa[here] = r.xsa[...]
+
+    @pl.when((core == 0) | (low == 0))
+    def _():
+        send(r.xsa, slot, r.e_s.at[0], r.e_r.at[low], there)
+
+    def rows_of(d):
+        return r.xa.at[pl.ds(pl.multiple_of(d * rows, rows), rows)]
+
+    for side in range(2):
+        rows_from = high * 2 + side
+
+        @pl.when((core == 1) & ((low == 0) | (side == 0)))
+        def _():
+            await_bytes(rows_of(rows_from), r.e_r.at[side])
+
+        @pl.when(core == 1)
+        def _():
+            for k in range(1, n):
+                part = rows_of(rows_from)
+                send(part, part, r.f_s.at[side, k], r.f_r.at[side, k], (lax.rem(high + k, n) * 2 + low, tensor))
+
+    for g in gathers:
+        g.forward()
+    for g in gathers:
+        g.finish()
+
+    @pl.when(core == 1)
+    def _():
+        for t, s in ((tensor, 0), (tensor ^ 2, 1)):
+            block = r.xmat.at[:, cols(t)]
+            send(block, block, r.j_s.at[s], r.j_r.at[s], (data, tensor ^ 1))
+
+    @pl.when(core == 1)
+    def _():
+        for side in range(2):
+            for k in range(1, n):
+                part = rows_of(lax.rem(high + n - k, n) * 2 + side)
+                await_bytes(part, r.f_r.at[side, k])
+                await_bytes(part, r.f_s.at[side, k])
+        for s in range(2):
+            await_bytes(r.xmat.at[:, cols(0)], r.j_s.at[s])
+
+    @pl.when(core == 0)
+    def _():
+        for s in range(2):
+            await_bytes(r.xmat.at[:, cols(0)], r.j_r.at[s])
+
+    await_bytes(r.xsd, r.swap_s)
+    out_low.wait_send()
+
+    @pl.when(high != tensor)
+    def _():
+        await_bytes(r.osend, r.o_s.at[1])
+
+    @pl.when((high == tensor) & (tensor != 3))
+    def _():
+        await_bytes(r.oout, r.o_s.at[2])
+
+    for m in range(3):
+
+        @pl.when(tensor != m)
+        def _():
+            await_bytes(r.asend.at[m], r.a_s.at[m])
+
+    @pl.when((core == 0) | (low == 0))
+    def _():
+        await_bytes(r.xsa, r.e_s.at[0])
+
+    finish_partials()
+
+
+def reduce_and_gather(count, rows, grads, attn_mom, up_mom, down_mom):
+    v = pltpu.VMEM
+    n = count // 2
+    scratch = dict(
+        pbuf=v((TENSOR, 4, 768), F32),
+        psum=v((4, 768), F32),
+        qbuf=v((count, 4, 768), F32),
+        pt_s=dma(4),
+        pt_r=dma(4),
+        pd_s=dma(count),
+        pd_r=dma(count),
+        olow=v((rows, 768), BF),
+        osend=v((rows, 768), BF),
+        ohigh=v((n, rows, 768), BF),
+        oout=v((rows, 768), BF),
+        oin=v((rows, 768), BF),
+        o_s=dma(3),
+        o_r=dma(n),
+        oin_r=pltpu.SemaphoreType.DMA,
+        xsd=v((rows, 768), BF),
+        xsu=v((rows, 768), BF),
+        xsa=v((rows, 768), BF),
+        swap_s=pltpu.SemaphoreType.DMA,
+        swap_r=pltpu.SemaphoreType.DMA,
+        x_s=dma(count),
+        x_r=dma(count),
+        y_s=dma(count),
+        y_r=dma(count),
+        asend=v((3, rows, 256), BF),
+        abuf=v((TENSOR, rows, 256), BF),
+        a_s=dma(3),
+        a_r=dma(TENSOR),
+        grad_a=v((rows, 768), F32),
+        e_s=dma(1),
+        e_r=dma(2),
+        f_s=dma(2, n),
+        f_r=dma(2, n),
+        j_s=dma(2),
+        j_r=dma(2),
+    )
+    for key in "dua":
+        part = (3, rows, 256) if key == "a" else (rows, 768)
+        for name in ("low", "hs", "hb"):
+            scratch[name + key] = v((n,) + part, BF)
+        for name in ("ls_", "lr_", "hs_", "hr_"):
+            scratch[name + key] = dma(n)
+    return kernel_call(
+        functools.partial(reduce_body, count, rows),
+        "reduce_and_gather",
+        dict(
+            gu=grads["gu"],
+            gd=grads["gd"],
+            ga=grads["ga"],
+            go=grads["go"],
+            partial=grads["partial"],
+            attn_mom=attn_mom,
+            up_mom=up_mom,
+            down_mom=down_mom,
+        ),
+        dict(
+            mom_a=shape(rows, 768, dtype=F32),
+            mom_u=shape(rows, 768, dtype=F32),
+            mom_d=shape(rows, 768, dtype=F32),
+            norm_grad=shape(4, 768, dtype=F32),
+            xmat=shape(768, TENSOR * 768),
+            xa=shape(768, 768),
+        ),
+        scratch,
+        2,
+    )
+
+
+def square_sum(ref, width):
+    def step(k, total):
+        part = ref[pl.ds(pl.multiple_of(k * 96, 96), 96)].astype(F32)
+        return total + part * part
+
+    total = lax.fori_loop(0, 8, step, jnp.zeros((96, width), F32))
+    return jnp.sum(total)
+
+
+def newton(x, gram, poly, chunk):
+    width = x.shape[1]
+    start = 1.0 / (jnp.sqrt(square_sum(x, width)) + NS_EPS)
+    edges = [slice(k * 256, (k + 1) * 256) for k in range(3)]
+
+    def step(k, first):
+        scale = jnp.where(k == 0, first, 1.0)
+        for a in range(3):
+            for b in range(a, 3):
+                block = (nt(x[edges[a], :], x[edges[b], :]) * (scale * scale)).astype(BF)
+                gram[edges[a], edges[b]] = block
+                if b > a:
+                    gram[edges[b], edges[a]] = block.T
+        for a in range(3):
+            for b in range(a, 3):
+                block = COEF_C * nt(gram[edges[a], :], gram[edges[b], :])
+                block = (block + COEF_B * gram[edges[a], edges[b]].astype(F32)).astype(BF)
+                poly[edges[a], edges[b]] = block
+                if b > a:
+                    poly[edges[b], edges[a]] = block.T
+
+        def columns(c, carry):
+            at = pl.ds(pl.multiple_of(c * chunk, chunk), chunk)
+            old = x[:, at]
+            x[:, at] = (scale * (COEF_A * old.astype(F32) + nn(poly[...], old))).astype(BF)
+            return carry
+
+        lax.fori_loop(0, width // chunk, columns, 0)
+        return first
+
+    lax.fori_loop(0, NS_STEPS, step, start)
+
+
+def ortho_body(count, rows, r):
+    data, tensor = place()
+    far, core = tensor // 2, tensor % 2
+    high, low = data // 2, data % 2
+    other = high * 2 + 1 - low
+    greet([(data, tensor ^ k) for k in (1, 2, 3)] + [(other, tensor), (other, tensor ^ 1)])
+    here = pl.ds(pl.multiple_of(data * rows, rows), rows)
+    there = pl.ds(pl.multiple_of(other * rows, rows), rows)
+
+    def cols(t):
+        return pl.ds(pl.multiple_of(t * 768, 768), 768)
+
+    @pl.when(core == 0)
+    def _():
+        r.big[...] = r.xmat[...]
+        newton(r.big, r.gram, r.poly, 512)
+
+    @pl.when(core == 1)
+    def _():
+        r.small[...] = r.xa[...]
+        newton(r.small, r.gram, r.poly, 768)
+
+    for m, out, recv in ((0, r.o_u, 0), (1, r.o_d, 1)):
+
+        @pl.when((core == 0) & (far == m))
+        def _():
+            for k in (1, 2, 3):
+                send(r.big.at[here, cols(tensor ^ k)], out, r.w_s.at[k], r.w_r.at[recv], (data, tensor ^ k))
+            out[...] = r.big[here, cols(tensor)]
+
+        @pl.when((core == 1) | (far != m))
+        def _():
+            await_bytes(out, r.w_r.at[recv])
+
+    owner = far * 2 + low
+
+    @pl.when((core == 1) & (low == 1))
+    def _():
+        r.o_a[...] = r.small[here]
+        send(r.small.at[there], r.o_a, r.v_s.at[0], r.v_r, (other, owner))
+
+    @pl.when((core == 1) & (low == 0))
+    def _():
+        send(r.small.at[here], r.o_a, r.v_s.at[0], r.v_r, (data, owner))
+        send(r.small.at[there], r.o_a, r.v_s.at[1], r.v_r, (other, owner))
+
+    @pl.when((core == 0) | (low == 0))
+    def _():
+        await_bytes(r.o_a, r.v_r)
+
+    @pl.when(core == 0)
+    def _():
+        for k in (1, 2, 3):
+            await_bytes(r.o_u, r.w_s.at[k])
+
+    @pl.when(core == 1)
+    def _():
+        await_bytes(r.o_a, r.v_s.at[0])
+
+    @pl.when((core == 1) & (low == 0))
+    def _():
+        await_bytes(r.o_a, r.v_s.at[1])
+
+
+def orthogonalize_all(count, rows, xmat, xa):
+    v = pltpu.VMEM
+    return kernel_call(
+        functools.partial(ortho_body, count, rows),
+        "orthogonalize",
+        dict(xmat=xmat, xa=xa),
+        dict(o_u=shape(rows, 768), o_d=shape(rows, 768), o_a=shape(rows, 768)),
+        dict(
+            big=v((768, TENSOR * 768), BF),
+            small=v((768, 768), BF),
+            gram=v((768, 768), BF),
+            poly=v((768, 768), BF),
+            w_s=dma(4),
+            w_r=dma(2),
+            v_s=dma(2),
+            v_r=pltpu.SemaphoreType.DMA,
+        ),
+        3,
+    )
+
+
+def step_on_device(
+    tokens,
+    cotangent,
+    lengths,
+    attn_w,
+    up_w,
+    down_w,
+    norm_params,
+    attn_mom,
+    up_mom,
+    down_mom,
+    norm_m1,
+    norm_m2,
+):
+    count = lax.axis_size("dp")
+    tensor = lax.axis_index("tensor")
+    rows = attn_w.shape[1]
+    length = lengths[0]
+    where = jnp.arange(TENSOR * QUARTER)
+    live = (where < length).astype(F32)
+    theta = 0.5 * math.pi * jnp.minimum(where, length - 1).astype(F32) / length.astype(F32)
+    table = jnp.where(
+        jnp.arange(LANES)[None, :] < HDIM, jnp.cos(theta)[:, None], jnp.sin(theta)[:, None]
+    )
+    table_live = (table * live[:, None]).reshape(TENSOR, QUARTER, LANES)
+    table = table.reshape(TENSOR, QUARTER, LANES)
+    live_rows = lax.dynamic_slice_in_dim(live, tensor * QUARTER, QUARTER, 0)[:, None]
+    shard = attn_w[0].astype(BF)
+    slabs = jnp.transpose(shard.reshape(rows, TENSOR, 192), (1, 0, 2))
+    slabs = jnp.pad(slabs, ((0, 0), (0, 0), (0, 64)))
+    gathered = gather_inputs(
+        count,
+        rows,
+        tokens,
+        slabs,
+        shard.reshape(2, rows // 2, 768),
+        up_w.astype(BF),
+        down_w.T.astype(BF),
+    )
+    grads = layer(
+        count,
+        rows,
+        gathered,
+        gathered["wo"].reshape(768, 768),
+        cotangent,
+        norm_params,
+        live_rows,
+        table,
+        table_live,
+    )
+    sums = reduce_and_gather(count, rows, grads, attn_mom[0], up_mom, down_mom.T)
+    orth = orthogonalize_all(count, rows, sums["xmat"], sums["xa"])
+    keep = 1.0 - MUON_RATE * MUON_DECAY
+    rate_a = MUON_RATE * 0.2 * math.sqrt(768)
+    rate_ff = MUON_RATE * 0.2 * math.sqrt(TENSOR * 768)
+    new_a = attn_w[0] * keep - rate_a * orth["o_a"].astype(F32)
+    new_u = up_w * keep - rate_ff * orth["o_u"].astype(F32)
+    new_d = down_w * keep - rate_ff * orth["o_d"].T.astype(F32)
+    norm_grad = sums["norm_grad"]
+    norm_moment1 = 0.5 * norm_m1 + 0.5 * norm_grad
+    norm_moment2 = 0.95 * norm_m2 + 0.05 * norm_grad * norm_grad
+    first_hat = norm_moment1 / (1.0 - 0.5**STEP)
+    second_hat = norm_moment2 / (1.0 - 0.95**STEP)
+    norm_new = norm_params - ADAM_RATE * first_hat / (jnp.sqrt(second_hat) + 1e-08)
+    return (
+        grads["mixed"],
+        grads["input_grad"],
+        new_a[None],
+        sums["mom_a"][None],
+        new_u,
+        sums["mom_u"],
+        new_d,
+        sums["mom_d"].T,
+        norm_moment1,
+        norm_moment2,
+        norm_new,
+    )
+
+
 def solution(mesh):
     placed = (
         P(("dp", "tensor"), None),
@@ -378,8 +1584,9 @@
         P(),
         P(),
     )
+    whole_tiles = mesh.shape["dp"] == 8 and mesh.shape["tensor"] == TENSOR
     return jax.shard_map(
-        on_device,
+        step_on_device if whole_tiles else on_device,
         mesh=mesh,
         in_specs=placed,
         out_specs=(

time: 936 us -> 373 us (0.40); the launches traced: 925 us -> 372 us
  waiting for transfers between devices: 399 us -> 0 us
  Pallas kernels: 0 us -> 355 us
  matrix products: 239 us -> 0 us
  local copies, waits for them, and re-layouts: 130 us -> 5.65 us
  other arithmetic: 88 us -> 9.65 us
  blocking collectives: 38.2 us -> 0 us
  between operations: 17.9 us -> 1.53 us
  starting transfers between devices: 12.1 us -> 0 us
    pallas_call x0 -> x4, Pallas kernels: none -> 355 us  [kernel_call(): pl.pallas_call(kernel, name=name, out_shape=[outs[n] for n in out_names],...]
    all_gather x12 -> x0, waiting for transfers between devices: 295 us -> none  [the longest x1 42.5 us: on_device(): lax.all_gather(start_u, 'dp', axis=0, tiled=True)]
    dot_general x49 -> x0, matrix products: 239 us -> none  [the longest x10 69.8 us: newton_update(): jnp.dot(poly, iterate, preferred_element_type=jnp.float32)]
    reduce_scatter x2 -> x0, waiting for transfers between devices: 53.1 us -> none  [the longest x1 27.2 us: on_device(): lax.psum_scatter(contract_cols(grad_pre, up_block).astype(jnp.bfloat16),...]
    all_to_all x2 -> x0, waiting for transfers between devices: 50.6 us -> none  [sum_at_owner(): pieces = lax.all_to_all(cut_along(array, dim, size), axis, 0, 0, tiled=True)]
    psum x1 -> x0, blocking collectives: 38.2 us -> none  [on_device(): totals, norm_grad = lax.psum((squares, norm_partial), ('dp', 'tensor'))]
    unnamed x136 -> x33, local copies, waits for them, and re-layouts: 36.3 us -> 3.84 us
    reshape x6 -> x0, local copies, waits for them, and re-layouts: 27.9 us -> none  [the longest x4 20.6 us: features(): soft = jax.nn.softplus(proj).reshape(count, HEADS, HDIM)]
  transfers between devices with their start and end apart: 17 -> 0, of which waited for: 13 -> 0; matrix products, arithmetic and copies ran while one was open for 35% -> 0% of each run, Pallas kernels for 0% -> 0%
where the time goes in v1:
time: 373 us; the launch traced here: 372 us
  Pallas kernels  355 us (95%)
  other arithmetic  9.65 us (3%)
  local copies, waits for them, and re-layouts  5.65 us (2%)
    pallas_call x4, Pallas kernels, kernel_call(): pl.pallas_call(kernel, name=name, out_shape=[outs[n] for n in out_names],...  355 us

profile of v1, /device:TPU:1, one launch (start us, length us, event | category | flops | bytes accessed | tf_op | source)
XLA Modules:
  0.0 371.7 jit_solution(7541472840887831962)
XLA Ops:
  0.6 0.0 copy-start.3
  1.4 0.1 dynamic_slice.3
  1.5 0.1 fusion.5
  1.5 0.8 copy.24.refs_7_
  2.3 1.0 convert_element_type.53
  3.3 0.0 copy-start
  3.3 1.7 convert_element_type.56.refs_3_
  5.0 0.0 copy-done.3
  5.0 0.7 convert_bitcast_fusion.refs_4_
  5.7 0.2 convert_element_type.54
  5.9 0.7 pad.4.refs_1_
  6.6 1.4 broadcast_multiply_fusion
  8.1 0.0 copy-done
  8.1 78.4 %gather_inputs.1 = (bf16[4,256,768]{2,1,0:T(8,128)(2,1)}, bf16[8,3,96,256]{3,2,1,0:T(8,128)(2,1)}, bf16[8,2,48,768]{3,2,1,0:T(8,128)(2,1)}, bf16[8,96,768]{2,1,0:T(8,128)(2,1)}, bf16[8,96,768]{2,1,0:T(8,128)(2,1)}) custom-call(bf16[256,768]{1,0:T(8,128)(2,1)} %refs_0_.1, bf16[4,96,256]{2,1,0:T(8,128)(2,1)} %pad.4.refs_1_, bf16[2,48,768]{2,1,0:T(8,128)(2,1)} %bitcast.25, ...), custom_call_target="tpu_custom_call" | custom-call | tf_op jit(solution)/shard_map/gather_inputs/pallas_call | solution.py:435
  86.4 106.2 %layer.1 = (bf16[256,768]{1,0:T(8,128)(2,1)}, f32[256,768]{1,0:T(8,128)}, bf16[8,96,768]{2,1,0:T(8,128)(2,1)}, bf16[8,96,768]{2,1,0:T(8,128)(2,1)}, bf16[8,3,96,...) custom-call(bf16[4,256,768]{2,1,0:T(8,128)(2,1)} %get-tuple-element.32.refs_0_, ...), custom_call_target="tpu_custom_call" | custom-call | tf_op jit(solution)/shard_map/layer/pallas_call | solution.py:435
  192.6 107.7 %reduce_and_gather.1 = (f32[96,768]{1,0:T(8,128)}, f32[96,768]{1,0:T(8,128)}, f32[96,768]{1,0:T(8,128)}, f32[4,768]{1,0:T(4,128)}, bf16[768,3072]{1,0:T(8,128)(2,1)}, /*index=5*/bf16[768,768]{1,0:T(8,128)(2,1)}) custom-call(bf16[8,96,768]{2,1,0:T(8,128)(2,1)} %get-tuple-element.39.refs_0_, bf16[8,96,768]{2,1,0:T(8,128)(2,1)} %get-tuple-element.40.refs_1_, ...), custom_call_target="tpu_custom_call" | custom-call | tf_op jit(solution)/shard_map/reduce_and_gather/pallas_call | solution.py:435
  300.3 0.0 copy-start.10
  300.4 0.0 copy-start.11
  300.4 0.0 copy-start.12
  300.4 0.0 copy-start.13
  300.4 0.0 copy-start.1
  300.4 0.0 copy-start.2
  300.4 62.6 %orthogonalize.1 = (bf16[96,768]{1,0:T(8,128)(2,1)}, bf16[96,768]{1,0:T(8,128)(2,1)}, bf16[96,768]{1,0:T(8,128)(2,1)}) custom-call(bf16[768,3072]{1,0:T(8,128)(2,1)} %get-tuple-element.44.refs_0_, bf16[768,768]{1,0:T(8,128)(2,1)} %get-tuple-element.45.refs_1_), custom_call_target="tpu_custom_call" | custom-call | tf_op jit(solution)/shard_map/orthogonalize/pallas_call | solution.py:435
  363.0 0.0 copy-start.9
  363.1 0.0 copy-start.5
  363.1 0.0 copy-done.10
  363.1 0.0 copy-done.11
  363.1 0.0 copy-done.12
  363.1 0.0 copy-done.13
  363.1 0.6 divide_subtract_fusion
  363.7 0.0 copy-done.1
  363.7 1.7 fusion
  365.4 0.0 copy-done.2
  365.4 0.0 copy-start.4
  365.4 1.7 multiply_subtract_fusion
  367.2 0.0 copy-done.9
  367.2 0.8 bitcast_subtract_fusion
  367.9 0.0 copy-done.5
  367.9 0.0 copy-start.8
  367.9 0.7 copy.33
  368.7 0.0 copy-done.4
  368.7 0.9 copy.34
  369.6 0.0 copy-done.8
  369.6 0.7 copy.35
  370.3 0.0 copy-done.7
  370.3 0.7 copy.36
  371.0 0.0 copy-done.6
  371.0 0.7 copy.37
  (6 shorter events, 0.0 us)
Async XLA Ops:
  0.6 4.4 %copy-start.3 = (f32[768,96]{0,1:T(8,128)S(1)}, f32[768,96]{0,1:T(8,128)}, u32[]{:S(2)}) copy-start(f32[768,96]{0,1:T(8,128)} %param.17) | copy-start | bytes 884740
  3.3 4.8 %copy-start = (bf16[1,96,768]{2,1,0:T(8,128)(2,1)}, bf16[1,96,768]{2,1,0:T(8,128)(2,1)S(1)}, u32[]{:S(2)}) copy-start(bf16[1,96,768]{2,1,0:T(8,128)(2,1)S(1)} %convert_element_type.53) | copy-start | bytes 442372
  300.3 62.7 %copy-start.10 = (f32[4,768]{1,0:T(4,128)S(1)}, f32[4,768]{1,0:T(4,128)}, u32[]{:S(2)}) copy-start(f32[4,768]{1,0:T(4,128)} %refs_6_.2) | copy-start | bytes 36868
  300.4 62.7 %copy-start.11 = (f32[4,768]{1,0:T(4,128)S(1)}, f32[4,768]{1,0:T(4,128)}, u32[]{:S(2)}) copy-start(f32[4,768]{1,0:T(4,128)} %param.22) | copy-start | bytes 36868
  300.4 62.7 %copy-start.12 = (f32[4,768]{1,0:T(4,128)S(1)}, f32[4,768]{1,0:T(4,128)}, u32[]{:S(2)}) copy-start(f32[4,768]{1,0:T(4,128)} %param.23) | copy-start | bytes 36868
  300.4 62.7 %copy-start.13 = (f32[4,768]{1,0:T(4,128)S(1)}, f32[4,768]{1,0:T(4,128)}, u32[]{:S(2)}) copy-start(f32[4,768]{1,0:T(4,128)} %get-tuple-element.52) | copy-start | bytes 36868
  300.4 63.4 %copy-start.1 = (f32[1,96,768]{2,1,0:T(8,128)S(1)}, f32[1,96,768]{2,1,0:T(8,128)}, u32[]{:S(2)}) copy-start(f32[1,96,768]{2,1,0:T(8,128)} %param.15) | copy-start | bytes 884740
  300.4 65.0 %copy-start.2 = (f32[96,768]{1,0:T(8,128)S(1)}, f32[96,768]{1,0:T(8,128)}, u32[]{:S(2)}) copy-start(f32[96,768]{1,0:T(8,128)} %param.16) | copy-start | bytes 884740
  363.0 4.1 %copy-start.9 = (bf16[96,768]{1,0:T(8,128)(2,1)S(1)}, bf16[96,768]{1,0:T(8,128)(2,1)}, u32[]{:S(2)}) copy-start(bf16[96,768]{1,0:T(8,128)(2,1)} %get-tuple-element.50) | copy-start | bytes 442372
  363.1 4.9 %copy-start.5 = (bf16[256,768]{1,0:T(8,128)(2,1)S(1)}, bf16[256,768]{1,0:T(8,128)(2,1)}, u32[]{:S(2)}) copy-start(bf16[256,768]{1,0:T(8,128)(2,1)} %get-tuple-element.71) | copy-start | bytes 1179652
  365.4 3.3 copy-start.4
  367.9 1.6 copy-start.8
  368.7 1.6 copy-start.7
  368.7 2.3 copy-start.6

commit v2 on v0

--- a/solution.py
+++ b/solution.py
@@ -1,8 +1,12 @@
+import functools
 import math
+import types
 
 import jax
 import jax.numpy as jnp
 from jax import lax
+from jax.experimental import pallas as pl
+from jax.experimental.pallas import tpu as pltpu
 from jax.sharding import PartitionSpec as P
 
 HEADS = 12
@@ -363,6 +367,1127 @@
     )
 
 
+BF = jnp.bfloat16
+F32 = jnp.float32
+MESH = pl.DeviceIdType.MESH
+TENSOR = 4
+QUARTER = 256
+LANES = 128
+VMEM_LIMIT = 63 << 20
+GELU_C = math.sqrt(2.0 / math.pi)
+GELU_A = 0.044715
+
+
+def nn(left, right):
+    return jnp.dot(left, right, preferred_element_type=F32)
+
+
+def nt(left, right):
+    return lax.dot_general(left, right, (((1,), (1,)), ((), ())), preferred_element_type=F32)
+
+
+def tn(left, right):
+    return lax.dot_general(left, right, (((0,), (0,)), ((), ())), preferred_element_type=F32)
+
+
+def lanes_of(rows, cols=LANES):
+    return lax.broadcasted_iota(jnp.int32, (rows, cols), 1)
+
+
+def half_roll(array):
+    return pltpu.roll(array, LANES // 2, 1)
+
+
+def place():
+    data = lax.axis_index("dp")
+    tensor = lax.axis_index("tensor")
+    return data, tensor
+
+
+def greet(devices):
+    barrier = pltpu.get_barrier_semaphore()
+    for device in devices:
+        pl.semaphore_signal(barrier, inc=1, device_id=device, device_id_type=MESH)
+    pl.semaphore_wait(barrier, len(devices))
+
+
+def send(src, dst, send_sem, recv_sem, device):
+    copy = pltpu.make_async_remote_copy(
+        src_ref=src,
+        dst_ref=dst,
+        send_sem=send_sem,
+        recv_sem=recv_sem,
+        device_id=device,
+        device_id_type=MESH,
+    )
+    copy.start()
+    return copy
+
+
+def kernel_call(body, name, ins, outs, scratch, collective, scalars=()):
+    in_names = list(ins)
+    out_names = list(outs)
+    scratch_names = list(scratch)
+
+    def kernel(*refs):
+        body(types.SimpleNamespace(**dict(zip(in_names + out_names + scratch_names, refs))))
+
+    results = pl.pallas_call(
+        kernel,
+        name=name,
+        out_shape=[outs[n] for n in out_names],
+        in_specs=[
+            pl.BlockSpec(memory_space=pltpu.SMEM if n in scalars else pltpu.VMEM) for n in in_names
+        ],
+        out_specs=[pl.BlockSpec(memory_space=pltpu.VMEM)] * len(out_names),
+        scratch_shapes=[scratch[n] for n in scratch_names],
+        compiler_params=pltpu.CompilerParams(
+            collective_id=collective,
+            has_side_effects=collective is not None,
+            vmem_limit_bytes=VMEM_LIMIT,
+        ),
+    )(*[ins[n] for n in in_names])
+    return dict(zip(out_names, results))
+
+
+def shape(*dims, dtype=BF):
+    return jax.ShapeDtypeStruct(dims, dtype)
+
+
+def dma(*dims):
+    return pltpu.SemaphoreType.DMA(dims)
+
+
+def await_bytes(ref, sem):
+    pltpu.make_async_copy(ref, ref, sem).wait()
+
+
+class GatherDp:
+    def __init__(self, slot_of, sends, recvs, data, tensor, count):
+        self.slot_of, self.sends, self.recvs = slot_of, sends, recvs
+        self.data, self.tensor = data, tensor
+        self.n = count // 2
+        self.high, self.low = data // 2, data % 2
+        self.partner = (self.high * 2 + 1 - self.low, tensor)
+
+    def peer(self, step):
+        return lax.rem(self.high + step, self.n) * 2 + self.low
+
+    def start(self):
+        mine = self.slot_of(self.data)
+        self.along = []
+        for step in range(1, self.n):
+            to = (self.peer(step), self.tensor)
+            self.along.append(send(mine, mine, self.sends.at[step], self.recvs.at[step], to))
+        self.across = [send(mine, mine, self.sends.at[0], self.recvs.at[0], self.partner)]
+
+    def forward(self):
+        n = self.n
+        for step in range(1, n):
+            self.along[step - 1].wait_recv()
+            slot = self.slot_of(self.peer(n - step))
+            at = n - 1 + step
+            self.across.append(send(slot, slot, self.sends.at[at], self.recvs.at[at], self.partner))
+
+    def arrive(self):
+        for copy in self.across:
+            copy.wait_recv()
+
+    def close(self):
+        for copy in self.along + self.across:
+            copy.wait_send()
+
+
+def softplus_and_slope(x):
+    small = jnp.exp(-jnp.abs(x))
+    soft = jnp.maximum(x, 0.0) + jnp.log1p(small)
+    slope = jnp.where(x >= 0.0, 1.0, small) / (1.0 + small)
+    return soft, slope
+
+
+def spread_weights(r, matrices):
+    low = lanes_of(768) < 64
+    for m in matrices:
+        w = r.wqkv[:, m].reshape(768, 256)
+        first, second = w[:, :LANES].astype(F32), w[:, LANES:].astype(F32)
+        turned = half_roll(first)
+        if m < 2:
+            parts = [
+                jnp.where(low, first, turned),
+                jnp.where(low, turned, first),
+                jnp.where(low, second, half_roll(second)),
+            ]
+        else:
+            parts = [jnp.where(low, p, 0.0) for p in (first, turned, second)]
+        for h, part in enumerate(parts):
+            r.xmat[:, (3 * m + h) * LANES : (3 * m + h + 1) * LANES] = part.astype(BF)
+
+
+def project(r):
+    lane = lanes_of(QUARTER)
+
+    def step(q, carry):
+        both = nn(r.seq[q], r.xmat[:, : 9 * LANES])
+        table, table_live = r.gp[q, :, :LANES], r.gp[q, :, LANES : 2 * LANES]
+        for h in range(3):
+            soft, slope = softplus_and_slope(both[:, h * LANES : (h + 1) * LANES])
+            r.qf[h, q] = (soft * table).astype(BF)
+            r.qg[h, q] = slope * table
+            soft, slope = softplus_and_slope(both[:, (3 + h) * LANES : (4 + h) * LANES])
+            r.kf[h, q] = (soft * table_live).astype(BF)
+            r.kg[h, q] = slope * table_live
+            value = both[:, (6 + h) * LANES : (7 + h) * LANES]
+            ones = jnp.where((lane == 64) | (lane == 65), 1.0, 0.0)
+            r.va[h, q] = jnp.where(lane < 64, value, ones).astype(BF)
+        return carry
+
+    lax.fori_loop(0, TENSOR, step, 0)
+
+
+def attend(r, q):
+    lane = lanes_of(QUARTER)
+    keep = lanes_of(QUARTER, QUARTER) <= lax.broadcasted_iota(jnp.int32, (QUARTER, QUARTER), 0)
+
+    def head(h, carry):
+        qf, kf, va = r.qf[h, q], r.kf[h, q], r.va[h, q]
+        scores = jnp.where(keep, nt(qf, kf), 0.0).astype(BF)
+        r.sb[h, q] = scores
+        total = nn(scores, va)
+        if q > 0:
+            state = r.state[h].astype(BF)
+            r.st[h, q] = state
+            total = total + nn(qf, state)
+        if q < TENSOR - 1:
+            pairs = tn(kf, va)
+            r.state[h] = pairs if q == 0 else r.state[h] + pairs
+        inverse = 1.0 / total[:, 64:65]
+        r.af[h, q] = jnp.where(lane < 64, total * inverse, inverse)
+        return carry
+
+    lax.fori_loop(0, 3, head, 0)
+    zero, one, two = r.af[0, q], r.af[1, q], r.af[2, q]
+    r.attn[q, :, :LANES] = jnp.where(lane < 64, zero, half_roll(one)).astype(BF)
+    r.attn[q, :, LANES:] = jnp.where(lane < 64, two, 0.0).astype(BF)
+
+
+def norm_rows(resid):
+    center = resid - jnp.mean(resid, -1, keepdims=True)
+    spread = jnp.mean(center * center, -1, keepdims=True)
+    scale = lax.rsqrt(spread + NORM_EPS)
+    return center * scale, scale
+
+
+def norm_rows_back(normal, scale, grad):
+    return scale * (
+        grad
+        - jnp.mean(grad, -1, keepdims=True)
+        - normal * jnp.mean(grad * normal, -1, keepdims=True)
+    )
+
+
+class Group:
+    def __init__(self):
+        self.data, self.tensor = place()
+        self.far, self.core = self.tensor // 2, self.tensor % 2
+
+    def device(self, k):
+        return (self.data, self.tensor ^ k)
+
+
+def spread_quarter(r, g, buf, sends, recvs):
+    own = buf.at[g.tensor]
+    far = send(own, own, sends.at[0], recvs.at[0], g.device(2))
+    near = send(own, own, sends.at[1], recvs.at[1], g.device(1))
+
+    def arrived_near():
+        near.wait_recv()
+
+    def arrived_far():
+        far.wait_recv()
+        slot = buf.at[g.tensor ^ 2]
+        passed = send(slot, slot, sends.at[2], recvs.at[2], g.device(1))
+        passed.wait_recv()
+        for copy in (far, near, passed):
+            copy.wait_send()
+
+    return arrived_near, arrived_far
+
+
+class SumQuarters:
+    def __init__(self, r, g, slot):
+        self.r, self.g, self.slot, self.copies = r, g, slot, []
+
+    def near_out(self, j, value):
+        r, k = self.r, self.slot * 2 + j
+        r.near_send[j] = value.astype(BF)
+        self.copies.append(
+            send(r.near_send.at[j], r.near_recv.at[j], r.near_s.at[k], r.near_r.at[k], self.g.device(1))
+        )
+
+    def near_in(self, j, value):
+        self.copies[j].wait_recv()
+        return value + self.r.near_recv[j].astype(F32)
+
+    def far_out(self, value):
+        r, k = self.r, self.slot
+        r.far_send[...] = value.astype(BF)
+        self.far = send(r.far_send, r.far_recv, r.far_s.at[k], r.far_r.at[k], self.g.device(2))
+
+    def far_in(self, value):
+        self.far.wait_recv()
+        value = value + self.r.far_recv[...].astype(F32)
+        for copy in self.copies + [self.far]:
+            copy.wait_send()
+        return value
+
+
+def feed(r, q):
+    pre = nn(r.hb[q], r.wu[...].reshape(768, 768))
+    inner = jnp.tanh(GELU_C * (pre + GELU_A * pre * pre * pre))
+    half = 0.5 * (1.0 + inner)
+    r.gp[q] = half + 0.5 * pre * (1.0 - inner * inner) * (GELU_C * (1.0 + 3.0 * GELU_A * pre * pre))
+    hid = (pre * half).astype(BF)
+    r.hid[q] = hid
+    return nt(hid, r.wd[...].reshape(768, 768))
+
+
+def feed_back(r, q):
+    grad_act = nn(r.dr2[q], r.wd[...].reshape(768, 768))
+    grad_pre = (grad_act * r.gp[q]).astype(BF)
+    r.du[q] = grad_pre
+    return nt(grad_pre, r.wu[...].reshape(768, 768))
+
+
+def attend_back(r, g, q):
+    lane = lanes_of(QUARTER)
+    keep = lanes_of(QUARTER, QUARTER) <= lax.broadcasted_iota(jnp.int32, (QUARTER, QUARTER), 0)
+    dr1 = r.dr1[q]
+
+    def head(h, carry):
+        grad = nt(dr1, r.woh[h])
+        af = r.af[h, q]
+        inverse = af[:, 64:65]
+        dden = -jnp.sum(grad * af, -1, keepdims=True) * inverse
+        dden_low = dden.astype(BF).astype(F32)
+        extra = jnp.where(lane == 64, dden_low, jnp.where(lane == 65, dden - dden_low, 0.0))
+        dnum = jnp.where(lane < 64, grad * inverse, extra).astype(BF)
+        qf, kf, va, sb = r.qf[h, q], r.kf[h, q], r.va[h, q], r.sb[h, q]
+        ds = jnp.where(keep, nt(dnum, va), 0.0).astype(BF)
+        dqf = nn(ds, kf)
+        if q > 0:
+            dqf = dqf + nt(dnum, r.st[h, q])
+        dkf = tn(ds, qf)
+        dv = tn(sb, dnum)
+        if q < TENSOR - 1:
+            dkv = r.state[h].astype(BF)
+            dkf = dkf + nt(va, dkv)
+            dv = dv + nn(kf, dkv)
+        if q > 0:
+            pairs = tn(qf, dnum)
+            r.state[h] = pairs if q == TENSOR - 1 else r.state[h] + pairs
+        dqf = dqf * r.qg[h, q]
+        dkf = dkf * r.kg[h, q]
+        r.fold[0, h] = dqf + half_roll(dqf)
+        r.fold[1, h] = dkf + half_roll(dkf)
+        r.fold[2, h] = dv
+        return carry
+
+    lax.fori_loop(0, 3, head, 0)
+    for m in range(3):
+        second = r.fold[m, 1] if m < 2 else half_roll(r.fold[m, 1])
+        r.hb[q, :, 256 * m : 256 * m + LANES] = jnp.where(lane < 64, r.fold[m, 0], second).astype(BF)
+        r.hb[q, :, 256 * m + LANES : 256 * (m + 1)] = jnp.where(lane < 64, r.fold[m, 2], 0.0).astype(BF)
+    total = None
+    for m in range(3):
+        part = nt(r.hb[q, :, 256 * m : 256 * (m + 1)], r.wqkv[:, m].reshape(768, 256))
+        total = part if total is None else total + part
+    r.gp[q] = total
+
+
+class ReduceDp:
+    def __init__(self, src, low_buf, high_send, high_buf, sems, data, tensor, count):
+        self.src, self.low_buf, self.high_send, self.high_buf = src, low_buf, high_send, high_buf
+        self.low_s, self.low_r, self.high_s, self.high_r = sems
+        self.tensor, self.n = tensor, count // 2
+        self.high, self.low = data // 2, data % 2
+
+    def at(self, step):
+        return lax.rem(self.high + step, self.n)
+
+    def start(self):
+        partner = (self.high * 2 + 1 - self.low, self.tensor)
+        self.across = {}
+        for step in list(range(1, self.n)) + [0]:
+            h = self.at(step)
+            self.across[step] = send(
+                self.src.at[h * 2 + 1 - self.low],
+                self.low_buf.at[h],
+                self.low_s.at[step],
+                self.low_r.at[step],
+                partner,
+            )
+
+    def pair(self, step):
+        self.across[step].wait_recv()
+        h = self.at(step)
+        return self.src[h * 2 + self.low].astype(F32) + self.low_buf[h].astype(F32)
+
+    def forward(self):
+        self.along = []
+        for step in range(1, self.n):
+            self.high_send[step] = self.pair(step).astype(BF)
+            self.along.append(
+                send(
+                    self.high_send.at[step],
+                    self.high_buf.at[step],
+                    self.high_s.at[step],
+                    self.high_r.at[step],
+                    (self.at(step) * 2 + self.low, self.tensor),
+                )
+            )
+
+    def finish(self):
+        total = self.pair(0)
+        for step in range(1, self.n):
+            self.along[step - 1].wait_recv()
+            total = total + self.high_buf[step].astype(F32)
+        for copy in list(self.across.values()) + self.along:
+            copy.wait_send()
+        return total
+
+
+def assemble(r, core_rows):
+    low = lanes_of(core_rows) < 64
+    for pair in range(2):
+        even, odd = r.abuf[2 * pair].astype(F32), r.abuf[2 * pair + 1].astype(F32)
+        turned = half_roll(odd[:, :LANES])
+        base = 3 * LANES * pair
+        r.grad_a[:, base : base + LANES] = even[:, :LANES]
+        r.grad_a[:, base + LANES : base + 2 * LANES] = jnp.where(low, even[:, LANES:], turned)
+        r.grad_a[:, base + 2 * LANES : base + 3 * LANES] = jnp.where(low, turned, half_roll(odd[:, LANES:]))
+
+
+def square_sum(ref, width):
+    def step(k, total):
+        part = ref[pl.ds(pl.multiple_of(k * 96, 96), 96)].astype(F32)
+        return total + part * part
+
+    total = lax.fori_loop(0, 8, step, jnp.zeros((96, width), F32))
+    return jnp.sum(total)
+
+
+def newton(x, gram, poly, chunk):
+    width = x.shape[1]
+    start = 1.0 / (jnp.sqrt(square_sum(x, width)) + NS_EPS)
+    edges = [slice(k * 256, (k + 1) * 256) for k in range(3)]
+
+    def step(k, first):
+        scale = jnp.where(k == 0, first, 1.0)
+        for a in range(3):
+            for b in range(a, 3):
+                block = (nt(x[edges[a], :], x[edges[b], :]) * (scale * scale)).astype(BF)
+                gram[a, :, edges[b]] = block
+                if b > a:
+                    gram[b, :, edges[a]] = block.T
+        for a in range(3):
+            for b in range(a, 3):
+                block = COEF_C * nt(gram[a], gram[b])
+                block = (block + COEF_B * gram[a, :, edges[b]].astype(F32)).astype(BF)
+                poly[a, :, edges[b]] = block
+                if b > a:
+                    poly[b, :, edges[a]] = block.T
+
+        def columns(c, carry):
+            at = pl.ds(pl.multiple_of(c * chunk, chunk), chunk)
+            old = x[:, at]
+            x[:, at] = (scale * (COEF_A * old.astype(F32) + nn(poly[:3].reshape(768, 768), old))).astype(BF)
+            return carry
+
+        lax.fori_loop(0, width // chunk, columns, 0)
+        return first
+
+    lax.fori_loop(0, NS_STEPS, step, start)
+
+
+def angles(r):
+    rows = TENSOR * QUARTER
+    length = r.lengths[0]
+    where = lax.broadcasted_iota(jnp.int32, (rows, LANES), 0)
+    theta = 0.5 * math.pi * jnp.minimum(where, length - 1).astype(F32) / length.astype(F32)
+    table = jnp.where(lanes_of(rows) < 64, jnp.cos(theta), jnp.sin(theta))
+    live = jnp.where(where < length, 1.0, 0.0)
+    r.gp[:, :, :LANES] = table.reshape(TENSOR, QUARTER, LANES)
+    r.gp[:, :, LANES : 2 * LANES] = (table * live).reshape(TENSOR, QUARTER, LANES)
+
+
+def cut_heads(r, rows):
+    low = lanes_of(rows) < 64
+    tiles = [r.attn_w[0, :, k * LANES : (k + 1) * LANES] for k in range(6)]
+    for pair in range(2):
+        first, middle, last = tiles[3 * pair : 3 * pair + 3]
+        turned, rest = half_roll(middle), half_roll(last)
+        parts = [first, jnp.where(low, middle, 0.0), jnp.where(low, turned, rest), jnp.where(low, rest, 0.0)]
+        for k, part in enumerate(parts):
+            r.slabs[2 * pair + k // 2, :, (k % 2) * LANES : (k % 2 + 1) * LANES] = part.astype(BF)
+
+
+def assemble(r, core_rows):
+    low = lanes_of(core_rows) < 64
+    for pair in range(2):
+        even, odd = r.abuf[2 * pair].astype(F32), r.abuf[2 * pair + 1].astype(F32)
+        turned = half_roll(odd[:, :LANES])
+        base = 3 * LANES * pair
+        r.grad_a[:, base : base + LANES] = even[:, :LANES]
+        r.grad_a[:, base + LANES : base + 2 * LANES] = jnp.where(low, even[:, LANES:], turned)
+        r.grad_a[:, base + 2 * LANES : base + 3 * LANES] = jnp.where(low, turned, half_roll(odd[:, LANES:]))
+
+
+def step_body(count, rows, r):
+    g = Group()
+    data, tensor, far, core = g.data, g.tensor, g.far, g.core
+    high, low = data // 2, data % 2
+    other = high * 2 + 1 - low
+    n = count // 2
+    half = rows // 2
+    near_dev, far_dev = g.device(1), g.device(2)
+
+    cut_heads(r, rows)
+    r.wo_own[...] = r.attn_w[0].astype(BF).reshape(2, half, 768)
+    greet(
+        [g.device(k) for k in (1, 2, 3)]
+        + [(lax.rem(data + k, count), tensor) for k in range(1, count)]
+        + [(other, tensor ^ 1)]
+    )
+
+    for k in (1, 2, 3):
+        peer = tensor ^ k
+
+        @pl.when(tensor < 3)
+        def _():
+            send(r.slabs.at[peer], r.wqkv.at[data, tensor], r.slab_s.at[k], r.slab_r.at[tensor], g.device(k))
+
+        @pl.when(tensor == 3)
+        def _():
+            send(r.wo_own.at[peer % 2], r.wo.at[data, peer % 2], r.slab_s.at[k], r.slab_r.at[3], g.device(k))
+
+    r.seq[tensor] = r.tokens[...]
+    mine = r.seq.at[tensor]
+    tok_near = send(mine, mine, r.tok_s.at[0], r.tok_r.at[0], near_dev)
+    tok_far = send(mine, mine, r.tok_s.at[1], r.tok_r.at[1], far_dev)
+
+    @pl.when(tensor < 3)
+    def _():
+        r.wqkv[data, tensor] = r.slabs[tensor]
+
+    @pl.when(tensor == 3)
+    def _():
+        r.wo[data, core] = r.wo_own[core]
+
+    r.wu[data] = r.up_w[...].astype(BF)
+    r.wd[data] = r.down_w[...].astype(BF)
+
+    def gather(slot_of, key):
+        return GatherDp(slot_of, r.gather_s.at[key], r.gather_r.at[key], data, tensor, count)
+
+    heads = [gather(lambda d, m=m: r.wqkv.at[d, m], m) for m in range(3)]
+    outs = gather(lambda d: r.wo.at[d, core], 3)
+    ups = [gather(lambda d, k=k: r.wu.at[d, pl.ds(k * half, half)], 4 + k) for k in range(2)]
+    downs = [gather(lambda d, k=k: r.wd.at[d, pl.ds(k * half, half)], 6 + k) for k in range(2)]
+
+    for m in range(3):
+
+        @pl.when(tensor != m)
+        def _():
+            await_bytes(r.wqkv.at[data, m], r.slab_r.at[m])
+
+        heads[m].start()
+    angles(r)
+
+    @pl.when(tensor != 3)
+    def _():
+        await_bytes(r.wo.at[data, core], r.slab_r.at[3])
+
+    heads[0].forward()
+    outs.start()
+    tok_far.wait_recv()
+    slot = r.seq.at[tensor ^ 2]
+    tok_pass = send(slot, slot, r.tok_s.at[2], r.tok_r.at[2], near_dev)
+    heads[1].forward()
+    ups[0].start()
+    heads[2].forward()
+    ups[1].start()
+    for m in range(3):
+        heads[m].arrive()
+        spread_weights(r, [m])
+    tok_near.wait_recv()
+    tok_pass.wait_recv()
+    project(r)
+    outs.forward()
+    downs[0].start()
+    downs[1].start()
+
+    copies = [[], []]
+    for j in range(2):
+        attend(r, 2 * j)
+        attend(r, 2 * j + 1)
+        mine, rest = 2 * j + core, 2 * j + 1 - core
+        for k in (2, 1, 3):
+            quarter = mine if k == 2 else rest
+            copies[j].append(
+                send(r.attn.at[quarter], r.aall.at[tensor, j], r.attn_s.at[j, k], r.attn_r.at[j, k], g.device(k))
+            )
+        r.aall[tensor, j] = r.attn[mine]
+        ups[j].forward()
+
+    outs.arrive()
+    share = []
+    for d in range(count):
+        part = r.wo.at[d, core]
+        share.append(send(part, part, r.share_s.at[d], r.share_r.at[d], near_dev))
+    downs[0].forward()
+    for d in range(count):
+        part = r.wo.at[d, 1 - core]
+        await_bytes(part, r.share_r.at[d])
+    whole_out = r.wo[...].reshape(768, 768)
+    wop = [r.xmat.at[256 * t : 256 * (t + 1), 1536:2304] for t in range(3)] + [r.xmat.at[0:256, 2304:3072]]
+    for t in range(TENSOR):
+        wop[t][:192, :] = whole_out[192 * t : 192 * (t + 1)]
+        wop[t][192:, :] = jnp.zeros((64, 768), BF)
+    for t in range(TENSOR):
+
+        @pl.when(tensor == t)
+        def _():
+            for h in range(3):
+                r.woh[h, :64] = wop[t][64 * h : 64 * (h + 1), :]
+                r.woh[h, 64:] = jnp.zeros((64, 768), BF)
+
+    gain1, bias1, gain2, bias2 = (r.norms[k : k + 1] for k in range(4))
+    hs = []
+    for group_copies in copies:
+        for copy in group_copies:
+            copy.wait_recv()
+    for own in (False, True):
+        j = far if own else 1 - far
+        q = 2 * j + core
+        branch = nn(r.aall[0, j], wop[0][...])
+        for t in range(1, TENSOR):
+            branch = branch + nn(r.aall[t, j], wop[t][...])
+        normal, scale = norm_rows(r.seq[q].astype(F32) + branch)
+        hidden = normal * gain1 + bias1
+        r.hb[q] = hidden.astype(BF)
+        if own:
+            r.n1[...] = normal
+            r.s1[...] = jnp.broadcast_to(scale, (QUARTER, LANES))
+            r.h1[...] = hidden
+        hs.append(send(r.hb.at[q], r.hb.at[q], r.h_s.at[int(own)], r.h_r.at[int(own)], near_dev))
+    downs[1].forward()
+    for group_copies in copies:
+        for copy in group_copies:
+            copy.wait_send()
+
+    for part in ups + downs:
+        part.arrive()
+    total = SumQuarters(r, g, 0)
+    kept = feed(r, tensor ^ 2)
+    hs[0].wait_recv()
+    total.near_out(0, feed(r, tensor ^ 3))
+    total.far_out(total.near_in(0, kept))
+    hs[1].wait_recv()
+    total.near_out(1, feed(r, tensor ^ 1))
+    kept = feed(r, tensor)
+    for part in heads + [outs] + ups + downs:
+        part.close()
+    for copy in hs + share + [tok_near, tok_far, tok_pass]:
+        copy.wait_send()
+    for k in (1, 2, 3):
+
+        @pl.when(tensor < 3)
+        def _():
+            await_bytes(r.slabs.at[0], r.slab_s.at[k])
+
+        @pl.when(tensor == 3)
+        def _():
+            await_bytes(r.wo_own.at[0], r.slab_s.at[k])
+
+    kept = total.far_in(total.near_in(1, kept))
+
+    n2, s2 = norm_rows(r.h1[...] + kept)
+    row = lax.broadcasted_iota(jnp.int32, (QUARTER, 1), 0) + tensor * QUARTER
+    live = jnp.where(row < r.lengths[0], 1.0, 0.0)
+    r.mixed[...] = (live * (n2 * gain2 + bias2)).astype(BF)
+    dy = live * r.cotangent[...].astype(F32)
+    r.partial[2:3] = jnp.sum(dy * n2, 0, keepdims=True)
+    r.partial[3:4] = jnp.sum(dy, 0, keepdims=True)
+    dr2 = norm_rows_back(n2, s2, dy * gain2)
+    r.dr2f[...] = dr2
+    r.dr2[tensor] = dr2.astype(BF)
+    near, distant = spread_quarter(r, g, r.dr2, r.dr2_s, r.dr2_r)
+
+    sums = {}
+    for key in "dua":
+        sums[key] = ReduceDp(
+            *(getattr(r, name + key) for name in ("g", "low", "hs", "hb")),
+            [getattr(r, name + key) for name in ("ls_", "lr_", "hs_", "hr_")],
+            data,
+            tensor,
+            count,
+        )
+    total = SumQuarters(r, g, 1)
+    r.dh[...] = feed_back(r, tensor)
+    near()
+    total.near_out(0, feed_back(r, tensor ^ 1))
+    distant()
+    total.near_out(1, feed_back(r, tensor ^ 3))
+    total.far_out(total.near_in(1, feed_back(r, tensor ^ 2)))
+    grad = tn(r.dr2[...].reshape(1024, 768), r.hid[...].reshape(1024, 768))
+    r.gd[...] = grad.astype(BF).reshape(r.gd.shape)
+    sums["d"].start()
+    grad = tn(r.hb[...].reshape(1024, 768), r.du[...].reshape(1024, 768))
+    r.gu[...] = grad.astype(BF).reshape(r.gu.shape)
+    sums["u"].start()
+    r.dh[...] = total.near_in(0, r.dh[...]) + r.dr2f[...]
+    sums["d"].forward()
+    dh = total.far_in(r.dh[...])
+
+    n1 = r.n1[...]
+    r.partial[0:1] = jnp.sum(dh * n1, 0, keepdims=True)
+    r.partial[1:2] = jnp.sum(dh, 0, keepdims=True)
+    dr1 = norm_rows_back(n1, r.s1[:, :1], dh * gain1)
+    r.dr1f[...] = dr1
+    r.dr1[tensor] = dr1.astype(BF)
+    near, distant = spread_quarter(r, g, r.dr1, r.dr1_s, r.dr1_r)
+    r.pbuf[tensor] = r.partial[...]
+    parts = []
+    for k in (1, 2, 3):
+        parts.append(send(r.partial, r.pbuf.at[tensor], r.pt_s.at[k], r.pt_r.at[k], g.device(k)))
+    near()
+    sums["u"].forward()
+    distant()
+
+    attend_back(r, g, 3)
+    for copy in parts:
+        copy.wait()
+    r.psum[...] = ((r.pbuf[0] + r.pbuf[1]) + r.pbuf[2]) + r.pbuf[3]
+    r.qbuf[data] = r.psum[...]
+    parts = []
+    for k in range(1, count):
+        to = (lax.rem(data + k, count), tensor)
+        parts.append(send(r.psum, r.qbuf.at[data], r.pd_s.at[k], r.pd_r.at[k], to))
+    attend_back(r, g, 2)
+    here = pl.ds(pl.multiple_of(data * rows, rows), rows)
+    there = pl.ds(pl.multiple_of(other * rows, rows), rows)
+
+    def rows_of(d):
+        return pl.ds(pl.multiple_of(d * rows, rows), rows)
+
+    def cols(t):
+        return pl.ds(pl.multiple_of(t * 768, 768), 768)
+
+    moment = 0.5 * r.down_mom[...] + sums["d"].finish()
+    r.mom_d[...] = moment
+    r.xsd[...] = moment.astype(BF)
+    moment = 0.5 * r.up_mom[...] + sums["u"].finish()
+    r.mom_u[...] = moment
+    r.xsu[...] = moment.astype(BF)
+    own = r.xmat.at[here, cols(tensor)]
+
+    @pl.when(far == 0)
+    def _():
+        r.xmat[here, cols(tensor)] = r.xsu[...]
+        send(r.xsd, own, r.swap_s, r.swap_r, far_dev)
+
+    @pl.when(far == 1)
+    def _():
+        r.xmat[here, cols(tensor)] = r.xsd[...]
+        send(r.xsu, own, r.swap_s, r.swap_r, far_dev)
+
+    blocks = [
+        GatherDp(lambda d: r.xmat.at[rows_of(d), cols(tensor)], r.x_s.at[0], r.x_r.at[0], data, tensor, count),
+        GatherDp(lambda d: r.xmat.at[rows_of(d), cols(tensor ^ 2)], r.x_s.at[1], r.x_r.at[1], data, tensor, count),
+    ]
+    blocks[0].start()
+    attend_back(r, g, 1)
+    await_bytes(r.xmat.at[here, cols(tensor ^ 2)], r.swap_r)
+    blocks[1].start()
+    attend_back(r, g, 0)
+
+    grad = tn(r.seq[...].reshape(1024, 768), r.hb[...].reshape(1024, 768)).astype(BF)
+    for m in range(3):
+        r.ga[:, m] = grad[:, 256 * m : 256 * (m + 1)].reshape(count, rows, 256)
+    sums["a"].start()
+    grad = tn(r.attn[...].reshape(1024, 256), r.dr1[...].reshape(1024, 768)).astype(BF)
+    r.go[...] = grad[:192].reshape(r.go.shape)
+    out_low = send(r.go.at[1 - low], r.olow, r.o_s.at[0], r.o_r.at[0], (other, tensor))
+    total = SumQuarters(r, g, 2)
+    total.near_out(0, r.gp[tensor ^ 3])
+    total.near_out(1, r.gp[tensor ^ 1])
+    total.far_out(total.near_in(0, r.gp[tensor ^ 2]))
+    blocks[0].forward()
+    sums["a"].forward()
+
+    out_low.wait_recv()
+    r.grad_a[...] = r.go[low].astype(F32) + r.olow[...].astype(F32)
+    r.osend[...] = r.grad_a[...].astype(BF)
+    for k in range(1, n):
+
+        @pl.when(lax.rem(high + k, n) == tensor)
+        def _():
+            send(r.osend, r.ohigh.at[k], r.o_s.at[1], r.o_r.at[k], (tensor * 2 + low, tensor))
+
+    blocks[1].forward()
+    r.input_grad[...] = total.far_in(total.near_in(1, r.gp[tensor])) + r.dr1f[...]
+
+    summed = sums["a"].finish()
+    for m in range(3):
+        r.asend[m] = summed[m].astype(BF)
+    for m in range(3):
+
+        @pl.when(tensor != m)
+        def _():
+            send(r.asend.at[m], r.abuf.at[tensor], r.a_s.at[m], r.a_r.at[tensor], (data, m))
+
+        @pl.when(tensor == m)
+        def _():
+            r.abuf[tensor] = r.asend[m]
+
+    @pl.when(high == tensor)
+    def _():
+        whole = r.grad_a[...]
+        for k in range(1, n):
+            await_bytes(r.ohigh.at[k], r.o_r.at[k])
+            whole = whole + r.ohigh[k].astype(F32)
+        r.grad_a[...] = whole
+        r.oout[...] = whole.astype(BF)
+
+    @pl.when((high == tensor) & (tensor != 3))
+    def _():
+        send(r.oout, r.oin, r.o_s.at[2], r.oin_r, (data, 3))
+
+    @pl.when((tensor == 3) & (high != 3))
+    def _():
+        await_bytes(r.oin, r.oin_r)
+        r.grad_a[...] = r.oin[...].astype(F32)
+
+    for t in range(TENSOR):
+
+        @pl.when((tensor < 3) & (tensor != t))
+        def _():
+            await_bytes(r.abuf.at[t], r.a_r.at[t])
+
+    @pl.when(tensor < 3)
+    def _():
+        assemble(r, rows)
+
+    moment = 0.5 * r.attn_mom[0] + r.grad_a[...]
+    r.mom_a[...] = moment
+    r.xsa[...] = moment.astype(BF)
+
+    at_work = (high * 2 + core, far * 2 + 1)
+
+    @pl.when((core == 1) & (low == 1))
+    def _():
+        r.xa[here] = r.xsa[...]
+
+    @pl.when((core == 0) | (low == 0))
+    def _():
+        send(r.xsa, r.xa.at[here], r.e_s, r.e_r.at[low], at_work)
+
+    for side in range(2):
+        part = r.xa.at[rows_of(high * 2 + side)]
+
+        @pl.when((core == 1) & ((low == 0) | (side == 0)))
+        def _():
+            await_bytes(part, r.e_r.at[side])
+
+        @pl.when(core == 1)
+        def _():
+            for k in range(1, n):
+                to = (lax.rem(high + k, n) * 2 + low, tensor)
+                send(part, part, r.f_s.at[side, k], r.f_r.at[side, k], to)
+
+    for block in blocks:
+        block.arrive()
+        block.close()
+
+    @pl.when(core == 1)
+    def _():
+        for s, t in enumerate((tensor, tensor ^ 2)):
+            block = r.xmat.at[:, cols(t)]
+            send(block, block, r.j_s.at[s], r.j_r.at[s], near_dev)
+
+    for copy in parts:
+        copy.wait()
+    r.norm_grad[...] = sum((r.qbuf[d] for d in range(1, count)), r.qbuf[0])
+
+    @pl.when(core == 0)
+    def _():
+        for s in range(2):
+            await_bytes(r.xmat.at[:, cols(0)], r.j_r.at[s])
+        newton(r.xmat, r.du, r.hid, 512)
+
+    @pl.when(core == 1)
+    def _():
+        for side in range(2):
+            for k in range(1, n):
+                await_bytes(r.xa.at[rows_of(lax.rem(high + n - k, n) * 2 + side)], r.f_r.at[side, k])
+                await_bytes(r.xa.at[here], r.f_s.at[side, k])
+        newton(r.xa, r.du, r.hid, 768)
+
+    for m, out in enumerate((r.o_u, r.o_d)):
+
+        @pl.when((core == 0) & (far == m))
+        def _():
+            for k in (1, 2, 3):
+                send(r.xmat.at[here, cols(tensor ^ k)], out, r.w_s.at[k], r.w_r.at[m], g.device(k))
+            out[...] = r.xmat[here, cols(tensor)]
+
+    owner = far * 2 + low
+
+    @pl.when((core == 1) & (low == 1))
+    def _():
+        r.o_a[...] = r.xa[here]
+        send(r.xa.at[there], r.o_a, r.v_s.at[0], r.v_r, (other, owner))
+
+    @pl.when((core == 1) & (low == 0))
+    def _():
+        send(r.xa.at[here], r.o_a, r.v_s.at[0], r.v_r, (data, owner))
+        send(r.xa.at[there], r.o_a, r.v_s.at[1], r.v_r, (other, owner))
+
+    @pl.when((core == 0) | (low == 0))
+    def _():
+        await_bytes(r.o_a, r.v_r)
+
+    for m, out in enumerate((r.o_u, r.o_d)):
+
+        @pl.when((core == 1) | (far != m))
+        def _():
+            await_bytes(out, r.w_r.at[m])
+
+    await_bytes(r.xsd, r.swap_s)
+    out_low.wait_send()
+
+    @pl.when(high != tensor)
+    def _():
+        await_bytes(r.osend, r.o_s.at[1])
+
+    @pl.when((high == tensor) & (tensor != 3))
+    def _():
+        await_bytes(r.oout, r.o_s.at[2])
+
+    for m in range(3):
+
+        @pl.when(tensor != m)
+        def _():
+            await_bytes(r.asend.at[m], r.a_s.at[m])
+
+    @pl.when((core == 0) | (low == 0))
+    def _():
+        await_bytes(r.xsa, r.e_s)
+
+    @pl.when(core == 0)
+    def _():
+        for k in (1, 2, 3):
+            await_bytes(r.o_u, r.w_s.at[k])
+
+    @pl.when(core == 1)
+    def _():
+        for s in range(2):
+            await_bytes(r.xmat.at[:, cols(0)], r.j_s.at[s])
+        await_bytes(r.o_a, r.v_s.at[0])
+
+    @pl.when((core == 1) & (low == 0))
+    def _():
+        await_bytes(r.o_a, r.v_s.at[1])
+
+
+def step_call(count, rows, ins):
+    v = pltpu.VMEM
+    n = count // 2
+    one = pltpu.SemaphoreType.DMA
+    outs = dict(
+        mixed=shape(QUARTER, 768),
+        input_grad=shape(QUARTER, 768, dtype=F32),
+        mom_a=shape(rows, 768, dtype=F32),
+        mom_u=shape(rows, 768, dtype=F32),
+        mom_d=shape(rows, 768, dtype=F32),
+        norm_grad=shape(4, 768, dtype=F32),
+        o_u=shape(rows, 768),
+        o_d=shape(rows, 768),
+        o_a=shape(rows, 768),
+    )
+    per_head = (3, TENSOR, QUARTER, LANES)
+    quarters = (TENSOR, QUARTER, 768)
+    scratch = dict(
+        slabs=v((TENSOR, rows, 256), BF),
+        wo_own=v((2, rows // 2, 768), BF),
+        seq=v(quarters, BF),
+        wqkv=v((count, 3, rows, 256), BF),
+        wo=v((count, 2, rows // 2, 768), BF),
+        wu=v((count, rows, 768), BF),
+        wd=v((count, rows, 768), BF),
+        woh=v((3, LANES, 768), BF),
+        slab_s=dma(4),
+        slab_r=dma(4),
+        tok_s=dma(3),
+        tok_r=dma(3),
+        share_s=dma(count),
+        share_r=dma(count),
+        gather_s=dma(8, count),
+        gather_r=dma(8, count),
+        qf=v(per_head, BF),
+        kf=v(per_head, BF),
+        va=v(per_head, BF),
+        qg=v(per_head, F32),
+        kg=v(per_head, F32),
+        af=v(per_head, F32),
+        sb=v((3, TENSOR, QUARTER, QUARTER), BF),
+        st=v((3, TENSOR, LANES, LANES), BF),
+        state=v((3, LANES, LANES), F32),
+        attn=v((TENSOR, QUARTER, 256), BF),
+        aall=v((TENSOR, 2, QUARTER, 256), BF),
+        fold=v((3, 3, QUARTER, LANES), F32),
+        attn_s=dma(2, 4),
+        attn_r=dma(2, 4),
+        hb=v(quarters, BF),
+        n1=v((QUARTER, 768), F32),
+        s1=v((QUARTER, LANES), F32),
+        h1=v((QUARTER, 768), F32),
+        hid=v(quarters, BF),
+        gp=v(quarters, F32),
+        du=v(quarters, BF),
+        dr2=v(quarters, BF),
+        dr2f=v((QUARTER, 768), F32),
+        dr1=v(quarters, BF),
+        dr1f=v((QUARTER, 768), F32),
+        dh=v((QUARTER, 768), F32),
+        near_send=v((2, QUARTER, 768), BF),
+        near_recv=v((2, QUARTER, 768), BF),
+        far_send=v((QUARTER, 768), BF),
+        far_recv=v((QUARTER, 768), BF),
+        near_s=dma(6),
+        near_r=dma(6),
+        far_s=dma(3),
+        far_r=dma(3),
+        h_s=dma(2),
+        h_r=dma(2),
+        dr2_s=dma(3),
+        dr2_r=dma(3),
+        dr1_s=dma(3),
+        dr1_r=dma(3),
+        gu=v((count, rows, 768), BF),
+        gd=v((count, rows, 768), BF),
+        ga=v((count, 3, rows, 256), BF),
+        go=v((2, rows, 768), BF),
+        partial=v((4, 768), F32),
+        pbuf=v((TENSOR, 4, 768), F32),
+        psum=v((4, 768), F32),
+        qbuf=v((count, 4, 768), F32),
+        pt_s=dma(4),
+        pt_r=dma(4),
+        pd_s=dma(count),
+        pd_r=dma(count),
+        olow=v((rows, 768), BF),
+        osend=v((rows, 768), BF),
+        ohigh=v((n, rows, 768), BF),
+        oout=v((rows, 768), BF),
+        oin=v((rows, 768), BF),
+        o_s=dma(3),
+        o_r=dma(n),
+        oin_r=one,
+        asend=v((3, rows, 256), BF),
+        abuf=v((TENSOR, rows, 256), BF),
+        a_s=dma(3),
+        a_r=dma(TENSOR),
+        grad_a=v((rows, 768), F32),
+        xsd=v((rows, 768), BF),
+        xsu=v((rows, 768), BF),
+        xsa=v((rows, 768), BF),
+        xmat=v((768, TENSOR * 768), BF),
+        xa=v((768, 768), BF),
+        swap_s=one,
+        swap_r=one,
+        x_s=dma(2, count),
+        x_r=dma(2, count),
+        e_s=one,
+        e_r=dma(2),
+        f_s=dma(2, n),
+        f_r=dma(2, n),
+        j_s=dma(2),
+        j_r=dma(2),
+        w_s=dma(4),
+        w_r=dma(2),
+        v_s=dma(2),
+        v_r=one,
+    )
+    for key in "dua":
+        part = (3, rows, 256) if key == "a" else (rows, 768)
+        for name in ("low", "hs", "hb"):
+            scratch[name + key] = v((n,) + part, BF)
+        for name in ("ls_", "lr_", "hs_", "hr_"):
+            scratch[name + key] = dma(n)
+    body = functools.partial(step_body, count, rows)
+    return kernel_call(body, "layer_step", ins, outs, scratch, 0, ("lengths",))
+
+
+def step_on_device(
+    tokens,
+    cotangent,
+    lengths,
+    attn_w,
+    up_w,
+    down_w,
+    norm_params,
+    attn_mom,
+    up_mom,
+    down_mom,
+    norm_m1,
+    norm_m2,
+):
+    count = lax.axis_size("dp")
+    rows = attn_w.shape[1]
+    done = step_call(
+        count,
+        rows,
+        dict(
+            lengths=lengths,
+            tokens=tokens,
+            cotangent=cotangent,
+            attn_w=attn_w,
+            up_w=up_w,
+            down_w=down_w.T,
+            norms=norm_params,
+            attn_mom=attn_mom,
+            up_mom=up_mom,
+            down_mom=down_mom.T,
+        ),
+    )
+    keep = 1.0 - MUON_RATE * MUON_DECAY
+    rate_a = MUON_RATE * 0.2 * math.sqrt(768)
+    rate_ff = MUON_RATE * 0.2 * math.sqrt(TENSOR * 768)
+    new_a = attn_w[0] * keep - rate_a * done["o_a"].astype(F32)
+    new_u = up_w * keep - rate_ff * done["o_u"].astype(F32)
+    new_d = down_w * keep - rate_ff * done["o_d"].T.astype(F32)
+    norm_grad = done["norm_grad"]
+    norm_moment1 = 0.5 * norm_m1 + 0.5 * norm_grad
+    norm_moment2 = 0.95 * norm_m2 + 0.05 * norm_grad * norm_grad
+    first_hat = norm_moment1 / (1.0 - 0.5**STEP)
+    second_hat = norm_moment2 / (1.0 - 0.95**STEP)
+    norm_new = norm_params - ADAM_RATE * first_hat / (jnp.sqrt(second_hat) + 1e-08)
+    return (
+        done["mixed"],
+        done["input_grad"],
+        new_a[None],
+        done["mom_a"][None],
+        new_u,
+        done["mom_u"],
+        new_d,
+        done["mom_d"].T,
+        norm_moment1,
+        norm_moment2,
+        norm_new,
+    )
+
+
 def solution(mesh):
     placed = (
         P(("dp", "tensor"), None),
@@ -378,8 +1503,9 @@
         P(),
         P(),
     )
+    whole_tiles = mesh.shape["dp"] == 8 and mesh.shape["tensor"] == TENSOR
     return jax.shard_map(
-        on_device,
+        step_on_device if whole_tiles else on_device,
         mesh=mesh,
         in_specs=placed,
         out_specs=(

time: 936 us -> 252 us (0.27); the launches traced: 925 us -> 250 us
  waiting for transfers between devices: 399 us -> 0 us
  Pallas kernels: 0 us -> 240 us
  matrix products: 239 us -> 0 us
  local copies, waits for them, and re-layouts: 130 us -> 4.92 us
  other arithmetic: 88 us -> 3.88 us
  blocking collectives: 38.2 us -> 0 us
  between operations: 17.9 us -> 1.39 us
  starting transfers between devices: 12.1 us -> 0 us
    all_gather x12 -> x0, waiting for transfers between devices: 295 us -> none  [the longest x1 42.5 us: on_device(): lax.all_gather(start_u, 'dp', axis=0, tiled=True)]
    pallas_call x0 -> x1, Pallas kernels: none -> 240 us  [kernel_call(): pl.pallas_call(kernel, name=name, out_shape=[outs[n] for n in out_names],...]
    dot_general x49 -> x0, matrix products: 239 us -> none  [the longest x10 69.8 us: newton_update(): jnp.dot(poly, iterate, preferred_element_type=jnp.float32)]
    reduce_scatter x2 -> x0, waiting for transfers between devices: 53.1 us -> none  [the longest x1 27.2 us: on_device(): lax.psum_scatter(contract_cols(grad_pre, up_block).astype(jnp.bfloat16),...]
    all_to_all x2 -> x0, waiting for transfers between devices: 50.6 us -> none  [sum_at_owner(): pieces = lax.all_to_all(cut_along(array, dim, size), axis, 0, 0, tiled=True)]
    psum x1 -> x0, blocking collectives: 38.2 us -> none  [on_device(): totals, norm_grad = lax.psum((squares, norm_partial), ('dp', 'tensor'))]
    unnamed x136 -> x33, local copies, waits for them, and re-layouts: 36.3 us -> 4.92 us
    reshape x6 -> x0, local copies, waits for them, and re-layouts: 27.9 us -> none  [the longest x4 20.6 us: features(): soft = jax.nn.softplus(proj).reshape(count, HEADS, HDIM)]
  transfers between devices with their start and end apart: 17 -> 0, of which waited for: 13 -> 0; matrix products, arithmetic and copies ran while one was open for 35% -> 0% of each run, Pallas kernels for 0% -> 0%
where the time goes in v2:
time: 252 us; the launch traced here: 250 us
  Pallas kernels  240 us (95%)
  local copies, waits for them, and re-layouts  4.92 us (2%)
  other arithmetic  3.88 us (2%)
    pallas_call x1, Pallas kernels, kernel_call(): pl.pallas_call(kernel, name=name, out_shape=[outs[n] for n in out_names],...  240 us

profile of v2, /device:TPU:1, one launch (start us, length us, event | category | flops | bytes accessed | tf_op | source)
XLA Modules:
  0.0 250.0 jit_solution(9503636676827325932)
XLA Ops:
  1.3 0.0 copy-start
  1.3 239.8 %layer_step.1 = (bf16[256,768]{1,0:T(8,128)(2,1)}, f32[256,768]{1,0:T(8,128)}, f32[96,768]{1,0:T(8,128)}, f32[96,768]{1,0:T(8,128)}, f32[96,768]{1,0:T(8,128)}, ...) custom-call(s32[1]{0:T(128)S(6)} %copy.28.refs_0_, ...), custom_call_target="tpu_custom_call" | custom-call | tf_op jit(solution)/shard_map/layer_step/pallas_call | solution.py:435
  241.1 0.0 copy-done
  241.1 0.0 copy-start.1
  241.1 0.0 copy-start.9
  241.2 0.0 copy-start.8
  241.2 1.7 fusion
  242.9 0.0 copy-done.1
  242.9 0.0 copy-done.9
  242.9 0.0 copy-start.2
  242.9 0.0 copy-start.10
  242.9 0.0 copy-start.11
  242.9 0.0 copy-start.12
  242.9 0.0 copy-start.13
  242.9 0.0 copy-start.4
  242.9 0.8 multiply_subtract_fusion
  243.7 0.0 copy-done.8
  243.7 0.1 copy-done.2
  243.9 0.0 copy-start.3
  243.9 0.8 bitcast_subtract_fusion
  244.6 0.0 copy-done.10
  244.6 0.0 copy-done.11
  244.6 0.0 copy-done.12
  244.6 0.0 copy-done.13
  244.6 0.6 divide_subtract_fusion
  245.3 0.0 copy-done.4
  245.3 0.7 copy.29
  246.0 0.0 copy-done.3
  246.0 0.0 copy-start.7
  246.0 0.9 copy.30
  246.9 0.2 copy-done.7
  247.1 0.0 copy-start.6
  247.1 0.7 copy.31
  247.9 0.4 copy-done.6
  248.2 0.0 copy-start.5
  248.2 0.7 copy.32
  248.9 0.4 copy-done.5
  249.3 0.7 copy.33
Async XLA Ops:
  1.3 239.8 %copy-start = (f32[1,96,768]{2,1,0:T(8,128)S(1)}, f32[1,96,768]{2,1,0:T(8,128)}, u32[]{:S(2)}) copy-start(f32[1,96,768]{2,1,0:T(8,128)} %refs_3_.1) | copy-start | bytes 884740
  241.1 1.8 copy-start.1
  241.1 1.8 copy-start.9
  241.2 2.6 %copy-start.8 = (bf16[96,768]{1,0:T(8,128)(2,1)S(1)}, bf16[96,768]{1,0:T(8,128)(2,1)}, u32[]{:S(2)}) copy-start(bf16[96,768]{1,0:T(8,128)(2,1)} %get-tuple-element.26) | copy-start | bytes 442372
  242.9 1.0 copy-start.2
  242.9 1.7 copy-start.10
  242.9 1.7 copy-start.11
  242.9 1.7 copy-start.12
  242.9 1.7 copy-start.13
  242.9 2.3 copy-start.4
  243.9 2.2 copy-start.3
  246.0 1.1 copy-start.7
  247.1 1.1 copy-start.6
  248.2 1.1 copy-start.5

commit v3 on v2

--- a/solution.py
+++ b/solution.py
@@ -767,28 +767,33 @@
         r.grad_a[:, base + 2 * LANES : base + 3 * LANES] = jnp.where(low, turned, half_roll(odd[:, LANES:]))
 
 
-def square_sum(ref, width):
+def newton_scale(x):
+    width = x.shape[1]
+
     def step(k, total):
-        part = ref[pl.ds(pl.multiple_of(k * 96, 96), 96)].astype(F32)
+        part = x[pl.ds(pl.multiple_of(k * 96, 96), 96)].astype(F32)
         return total + part * part
 
     total = lax.fori_loop(0, 8, step, jnp.zeros((96, width), F32))
-    return jnp.sum(total)
-
-
-def newton(x, gram, poly, chunk):
-    width = x.shape[1]
-    start = 1.0 / (jnp.sqrt(square_sum(x, width)) + NS_EPS)
+    return 1.0 / (jnp.sqrt(jnp.sum(total)) + NS_EPS)
+
+
+def newton_gram(x, gram, scale):
     edges = [slice(k * 256, (k + 1) * 256) for k in range(3)]
-
-    def step(k, first):
+    for a in range(3):
+        for b in range(a, 3):
+            block = (nt(x[edges[a], :], x[edges[b], :]) * (scale * scale)).astype(BF)
+            gram[a, :, edges[b]] = block
+            if b > a:
+                gram[b, :, edges[a]] = block.T
+
+
+def newton(x, gram, poly, chunk, first, begin, end):
+    edges = [slice(k * 256, (k + 1) * 256) for k in range(3)]
+
+    def step(k, carry):
         scale = jnp.where(k == 0, first, 1.0)
-        for a in range(3):
-            for b in range(a, 3):
-                block = (nt(x[edges[a], :], x[edges[b], :]) * (scale * scale)).astype(BF)
-                gram[a, :, edges[b]] = block
-                if b > a:
-                    gram[b, :, edges[a]] = block.T
+        newton_gram(x, gram, scale)
         for a in range(3):
             for b in range(a, 3):
                 block = COEF_C * nt(gram[a], gram[b])
@@ -797,16 +802,33 @@
                 if b > a:
                     poly[b, :, edges[a]] = block.T
 
-        def columns(c, carry):
+        def columns(c, inner):
             at = pl.ds(pl.multiple_of(c * chunk, chunk), chunk)
             old = x[:, at]
             x[:, at] = (scale * (COEF_A * old.astype(F32) + nn(poly[:3].reshape(768, 768), old))).astype(BF)
-            return carry
-
-        lax.fori_loop(0, width // chunk, columns, 0)
-        return first
-
-    lax.fori_loop(0, NS_STEPS, step, start)
+            return inner
+
+        lax.fori_loop(0, x.shape[1] // chunk, columns, 0)
+        return carry
+
+    lax.fori_loop(begin, end, step, 0)
+
+
+def newton_rows(x, gram, index, rows, chunk, out):
+    own = newton_rows_gram(gram, index, rows)
+    poly = (COEF_C * nn(own, gram[:3].reshape(768, 768)) + COEF_B * own.astype(F32)).astype(BF)
+    here = pl.ds(pl.multiple_of(index * rows, rows), rows)
+    for c in range(x.shape[1] // chunk):
+        at = slice(c * chunk, (c + 1) * chunk)
+        out[:, at] = (COEF_A * x[here, at].astype(F32) + nn(poly, x[:, at])).astype(BF)
+
+
+def newton_rows_gram(gram, index, rows):
+    parts = []
+    for k in range(rows // 32):
+        row = index * rows + 32 * k
+        parts.append(gram[row // 256, pl.ds(pl.multiple_of(lax.rem(row, 256), 32), 32), :])
+    return jnp.concatenate(parts, axis=0)
 
 
 def angles(r):
@@ -1105,6 +1127,13 @@
         GatherDp(lambda d: r.xmat.at[rows_of(d), cols(tensor)], r.x_s.at[0], r.x_r.at[0], data, tensor, count),
         GatherDp(lambda d: r.xmat.at[rows_of(d), cols(tensor ^ 2)], r.x_s.at[1], r.x_r.at[1], data, tensor, count),
     ]
+
+    def pass_on(b, d):
+        @pl.when(core == 1)
+        def _():
+            slot = blocks[b].slot_of(d)
+            send(slot, slot, r.j_s.at[b, d], r.j_r.at[b, d], near_dev)
+
     blocks[0].start()
     attend_back(r, g, 1)
     await_bytes(r.xmat.at[here, cols(tensor ^ 2)], r.swap_r)
@@ -1122,7 +1151,10 @@
     total.near_out(0, r.gp[tensor ^ 3])
     total.near_out(1, r.gp[tensor ^ 1])
     total.far_out(total.near_in(0, r.gp[tensor ^ 2]))
-    blocks[0].forward()
+    for b in range(2):
+        blocks[b].forward()
+        for step in range(n):
+            pass_on(b, blocks[b].peer(step))
     sums["a"].forward()
 
     out_low.wait_recv()
@@ -1134,8 +1166,21 @@
         def _():
             send(r.osend, r.ohigh.at[k], r.o_s.at[1], r.o_r.at[k], (tensor * 2 + low, tensor))
 
-    blocks[1].forward()
     r.input_grad[...] = total.far_in(total.near_in(1, r.gp[tensor])) + r.dr1f[...]
+
+    for b in range(2):
+        for step in range(n):
+            blocks[b].across[step].wait_recv()
+            pass_on(b, blocks[b].peer(n - step) + 1 - 2 * low if step else other)
+        blocks[b].close()
+
+    @pl.when(core == 0)
+    def _():
+        for b in range(2):
+            for d in range(count):
+                await_bytes(own, r.j_r.at[b, d])
+        r.scale[0] = newton_scale(r.xmat)
+        newton(r.xmat, r.du, r.hid, 512, r.scale[0], 0, 1)
 
     summed = sums["a"].finish()
     for m in range(3):
@@ -1205,25 +1250,25 @@
                 to = (lax.rem(high + k, n) * 2 + low, tensor)
                 send(part, part, r.f_s.at[side, k], r.f_r.at[side, k], to)
 
-    for block in blocks:
-        block.arrive()
-        block.close()
-
-    @pl.when(core == 1)
-    def _():
-        for s, t in enumerate((tensor, tensor ^ 2)):
-            block = r.xmat.at[:, cols(t)]
-            send(block, block, r.j_s.at[s], r.j_r.at[s], near_dev)
-
     for copy in parts:
         copy.wait()
     r.norm_grad[...] = sum((r.qbuf[d] for d in range(1, count)), r.qbuf[0])
 
     @pl.when(core == 0)
     def _():
-        for s in range(2):
-            await_bytes(r.xmat.at[:, cols(0)], r.j_r.at[s])
-        newton(r.xmat, r.du, r.hid, 512)
+        newton(r.xmat, r.du, r.hid, 512, 1.0, 1, NS_STEPS - 1)
+        newton_gram(r.xmat, r.du, 1.0)
+        newton_rows(r.xmat, r.du, data, rows, 768, r.orow)
+
+    for m, out in enumerate((r.o_u, r.o_d)):
+
+        @pl.when((core == 0) & (far == m))
+        def _():
+            for k in (1, 2, 3):
+                send(r.orow.at[:, cols(tensor ^ k)], out, r.w_s.at[k], r.w_r.at[m], g.device(k))
+            out[...] = r.orow[:, cols(tensor)]
+
+    owner = far * 2 + low
 
     @pl.when(core == 1)
     def _():
@@ -1231,27 +1276,19 @@
             for k in range(1, n):
                 await_bytes(r.xa.at[rows_of(lax.rem(high + n - k, n) * 2 + side)], r.f_r.at[side, k])
                 await_bytes(r.xa.at[here], r.f_s.at[side, k])
-        newton(r.xa, r.du, r.hid, 768)
-
-    for m, out in enumerate((r.o_u, r.o_d)):
-
-        @pl.when((core == 0) & (far == m))
-        def _():
-            for k in (1, 2, 3):
-                send(r.xmat.at[here, cols(tensor ^ k)], out, r.w_s.at[k], r.w_r.at[m], g.device(k))
-            out[...] = r.xmat[here, cols(tensor)]
-
-    owner = far * 2 + low
+        newton(r.xa, r.du, r.hid, 768, newton_scale(r.xa), 0, NS_STEPS - 1)
+        newton_gram(r.xa, r.du, 1.0)
+        newton_rows(r.xa, r.du, other, rows, 768, r.orow.at[:, 768:1536])
+        send(r.orow.at[:, 768:1536], r.o_a, r.v_s.at[0], r.v_r, (other, owner))
+        newton_rows(r.xa, r.du, data, rows, 768, r.orow.at[:, :768])
 
     @pl.when((core == 1) & (low == 1))
     def _():
-        r.o_a[...] = r.xa[here]
-        send(r.xa.at[there], r.o_a, r.v_s.at[0], r.v_r, (other, owner))
+        r.o_a[...] = r.orow[:, :768]
 
     @pl.when((core == 1) & (low == 0))
     def _():
-        send(r.xa.at[here], r.o_a, r.v_s.at[0], r.v_r, (data, owner))
-        send(r.xa.at[there], r.o_a, r.v_s.at[1], r.v_r, (other, owner))
+        send(r.orow.at[:, :768], r.o_a, r.v_s.at[1], r.v_r, (data, owner))
 
     @pl.when((core == 0) | (low == 0))
     def _():
@@ -1291,8 +1328,9 @@
 
     @pl.when(core == 1)
     def _():
-        for s in range(2):
-            await_bytes(r.xmat.at[:, cols(0)], r.j_s.at[s])
+        for b in range(2):
+            for d in range(count):
+                await_bytes(own, r.j_s.at[b, d])
         await_bytes(r.o_a, r.v_s.at[0])
 
     @pl.when((core == 1) & (low == 0))
@@ -1412,8 +1450,10 @@
         e_r=dma(2),
         f_s=dma(2, n),
         f_r=dma(2, n),
-        j_s=dma(2),
-        j_r=dma(2),
+        j_s=dma(2, count),
+        j_r=dma(2, count),
+        orow=v((rows, TENSOR * 768), BF),
+        scale=pltpu.SMEM((1,), F32),
         w_s=dma(4),
         w_r=dma(2),
         v_s=dma(2),
@@ -1427,6 +1467,48 @@
             scratch[name + key] = dma(n)
     body = functools.partial(step_body, count, rows)
     return kernel_call(body, "layer_step", ins, outs, scratch, 0, ("lengths",))
+
+
+def finish_body(r):
+    keep = 1.0 - MUON_RATE * MUON_DECAY
+    rate_a = MUON_RATE * 0.2 * math.sqrt(768)
+    rate_ff = MUON_RATE * 0.2 * math.sqrt(TENSOR * 768)
+    r.attn_new[0] = r.attn_w[0] * keep - rate_a * r.o_a[...].astype(F32)
+    r.up_new[...] = r.up_w[...] * keep - rate_ff * r.o_u[...].astype(F32)
+    r.down_new[...] = r.down_w[...] * keep - rate_ff * r.o_d[...].astype(F32)
+    r.attn_moment[0] = r.mom_a[...]
+    r.up_moment[...] = r.mom_u[...]
+    r.down_moment[...] = r.mom_d[...]
+    r.mixed_out[...] = r.mixed[...]
+    r.input_grad_out[...] = r.input_grad[...]
+    grad = r.norm_grad[...]
+    moment1 = 0.5 * r.norm_m1[...] + 0.5 * grad
+    moment2 = 0.95 * r.norm_m2[...] + 0.05 * grad * grad
+    first_hat = moment1 / (1.0 - 0.5**STEP)
+    second_hat = moment2 / (1.0 - 0.95**STEP)
+    r.norm_moment1[...] = moment1
+    r.norm_moment2[...] = moment2
+    r.norm_new[...] = r.norms[...] - ADAM_RATE * first_hat / (jnp.sqrt(second_hat) + 1e-08)
+
+
+def finish_call(ins):
+    rows = ins["up_w"].shape[0]
+    block = shape(rows, 768, dtype=F32)
+    small = shape(4, 768, dtype=F32)
+    outs = dict(
+        mixed_out=shape(QUARTER, 768),
+        input_grad_out=shape(QUARTER, 768, dtype=F32),
+        attn_new=shape(1, rows, 768, dtype=F32),
+        attn_moment=shape(1, rows, 768, dtype=F32),
+        up_new=block,
+        up_moment=block,
+        down_new=block,
+        down_moment=block,
+        norm_moment1=small,
+        norm_moment2=small,
+        norm_new=small,
+    )
+    return kernel_call(finish_body, "finish", ins, outs, {}, None)
 
 
 def step_on_device(
@@ -1461,30 +1543,29 @@
             down_mom=down_mom.T,
         ),
     )
-    keep = 1.0 - MUON_RATE * MUON_DECAY
-    rate_a = MUON_RATE * 0.2 * math.sqrt(768)
-    rate_ff = MUON_RATE * 0.2 * math.sqrt(TENSOR * 768)
-    new_a = attn_w[0] * keep - rate_a * done["o_a"].astype(F32)
-    new_u = up_w * keep - rate_ff * done["o_u"].astype(F32)
-    new_d = down_w * keep - rate_ff * done["o_d"].T.astype(F32)
-    norm_grad = done["norm_grad"]
-    norm_moment1 = 0.5 * norm_m1 + 0.5 * norm_grad
-    norm_moment2 = 0.95 * norm_m2 + 0.05 * norm_grad * norm_grad
-    first_hat = norm_moment1 / (1.0 - 0.5**STEP)
-    second_hat = norm_moment2 / (1.0 - 0.95**STEP)
-    norm_new = norm_params - ADAM_RATE * first_hat / (jnp.sqrt(second_hat) + 1e-08)
+    last = finish_call(
+        dict(
+            attn_w=attn_w,
+            up_w=up_w,
+            down_w=down_w.T,
+            norms=norm_params,
+            norm_m1=norm_m1,
+            norm_m2=norm_m2,
+            **done,
+        )
+    )
     return (
-        done["mixed"],
-        done["input_grad"],
-        new_a[None],
-        done["mom_a"][None],
-        new_u,
-        done["mom_u"],
-        new_d,
-        done["mom_d"].T,
-        norm_moment1,
-        norm_moment2,
-        norm_new,
+        last["mixed_out"],
+        last["input_grad_out"],
+        last["attn_new"],
+        last["attn_moment"],
+        last["up_new"],
+        last["up_moment"],
+        last["down_new"].T,
+        last["down_moment"].T,
+        last["norm_moment1"],
+        last["norm_moment2"],
+        last["norm_new"],
     )
 
 

time: 252 us -> 241 us (0.956)
  Pallas kernels: 240 us -> 235 us
  local copies, waits for them, and re-layouts: 4.92 us -> 0 us
  other arithmetic: 3.88 us -> 0 us
    unnamed x33 -> x0, local copies, waits for them, and re-layouts: 4.92 us -> none
    pallas_call x1 -> x2, Pallas kernels: 240 us -> 235 us  [kernel_call(): pl.pallas_call(kernel, name=name, out_shape=[outs[n] for n in out_names],...]
where the time goes in v3:
time: 241 us; the launch traced here: 237 us
  Pallas kernels  235 us (98%)
    pallas_call x2, Pallas kernels, kernel_call(): pl.pallas_call(kernel, name=name, out_shape=[outs[n] for n in out_names],...  235 us

profile of v3, /device:TPU:1, one launch (start us, length us, event | category | flops | bytes accessed | tf_op | source)
XLA Modules:
  0.0 236.9 jit_solution(2431152585793754771)
XLA Ops:
  1.3 231.6 %layer_step.1 = (bf16[256,768]{1,0:T(8,128)(2,1)}, f32[256,768]{1,0:T(8,128)}, f32[96,768]{1,0:T(8,128)}, f32[96,768]{1,0:T(8,128)}, f32[96,768]{1,0:T(8,128)}, ...) custom-call(s32[1]{0:T(128)S(6)} %copy.23.refs_0_, ...), custom_call_target="tpu_custom_call" | custom-call | tf_op jit(solution)/shard_map/layer_step/pallas_call | solution.py:435
  232.9 3.6 %finish.1 = (bf16[256,768]{1,0:T(8,128)(2,1)}, f32[256,768]{1,0:T(8,128)}, f32[1,96,768]{2,1,0:T(8,128)}, f32[1,96,768]{2,1,0:T(8,128)}, f32[96,768]{1,0:T(8,128...) custom-call(f32[1,96,768]{2,1,0:T(8,128)} %refs_0_.2, ...), custom_call_target="tpu_custom_call" | custom-call | tf_op jit(solution)/shard_map/finish/pallas_call | solution.py:435
